TPU v7x, 1024 devices: a whole 4x4x32 slice. The times are simulated.
1024 devices in a mesh: loop: 32 (over z_hi, x, core), group: 32 (over z_lo, y).
Axes of the slice: x: 4, y: 4, z: 32 (z_hi: 4, z_lo: 8; z = z_hi * 8 + z_lo), core: 2. Of those that a mesh axis runs over, the one named last changes fastest.
Arguments:
- images: bfloat16 [8192, 1152], P(('loop', 'group')), may hold values from -0.1875 to 0.1875
- texts: bfloat16 [8192, 1152], P(('loop', 'group')), may hold values from -0.1875 to 0.1875
- scale: float32 [], replicated, may hold values from 4 to 10
- bias: float32 [], replicated, may hold values from -3 to -1
Outputs:
- image_grad: float32 [8192, 1152], P(('loop', 'group'))
- text_grad: float32 [8192, 1152], P(('loop', 'group'))
- image_loss: float32 [8192], P(('loop', 'group'))
All inputs are finite; a program needn't handle non-finite values.
Results may differ from a plain program's by a relative error of at most 0.0044.
Values may be sent and summed in bfloat16 or wider, within the bound.
No kernel may reach another device: no remote copies, remote signals or barrier semaphores. Data moves between devices by JAX's collectives and lax.ppermute only.
A program may use at most 32 MiB of HBM per device.

v0:
```python
import jax
import jax.numpy as jnp
from jax import lax
from jax.sharding import PartitionSpec as P

ROUNDS = 3


EPS = 1e-06


def passed_along(value, axis, steps):
    count = lax.axis_size(axis)
    pairs = [(source, (source + steps) % count) for source in range(count)]
    return lax.ppermute(value, axis, pairs)


def normalize(x):
    xf = x.astype(jnp.float32)
    norms = jnp.sqrt(jnp.sum(xf * xf, axis=-1, keepdims=True) + EPS)
    return (xf / norms, norms)


def project_back(grad, unit, norms):
    return (grad - unit * jnp.sum(unit * grad, axis=-1, keepdims=True)) / norms


def on_device(images, texts, scale, bias):
    unit_img, norm_img = normalize(images)
    unit_txt, norm_txt = normalize(texts)
    img_half = unit_img.astype(jnp.bfloat16)
    txt_half = unit_txt.astype(jnp.bfloat16)
    rows = images.shape[0]
    member = lax.axis_index("group")
    pieces = []
    losses = jnp.zeros((rows,), jnp.float32)
    img_total = jnp.zeros(images.shape, jnp.float32)
    block = lax.all_gather(txt_half, "group", axis=0, tiled=True)
    for step in range(ROUNDS):
        if step > 0:
            block = passed_along(block, "loop", 1)
        logit = (
            scale * jnp.einsum("id,jd->ij", img_half, block, preferred_element_type=jnp.float32)
            + bias
        )
        if step == 0:
            column = lax.broadcasted_iota(jnp.int32, logit.shape, 1)
            row_ids = lax.broadcasted_iota(jnp.int32, logit.shape, 0)
            sign = jnp.where(column == member * rows + row_ids, 1.0, -1.0).astype(jnp.float32)
        else:
            sign = -jnp.ones_like(logit)
        losses = losses + jnp.sum(jax.nn.softplus(-sign * logit), axis=1)
        coef = (-sign * jax.nn.sigmoid(-sign * logit) * scale).astype(jnp.bfloat16)
        img_total = img_total + jnp.dot(coef, block, preferred_element_type=jnp.float32)

        def text_term(start, count, coef=coef):
            return jnp.einsum("ij,id->jd", coef, img_half, preferred_element_type=jnp.float32)

        pieces.append(
            lax.psum_scatter(
                text_term(jnp.int32(0), rows * lax.axis_size("group")),
                "group",
                scatter_dimension=0,
                tiled=True,
            )
        )
    gathered = pieces[ROUNDS - 1]
    for step in range(ROUNDS - 2, -1, -1):
        gathered = passed_along(gathered, "loop", -1) + pieces[step]
    image_grad = project_back(img_total, unit_img, norm_img)
    text_grad = project_back(gathered, unit_txt, norm_txt)
    return (image_grad, text_grad, losses)


def solution(mesh):
    in_specs = (P(("loop", "group"), None), P(("loop", "group"), None), P(), P())
    out_specs = (P(("loop", "group"), None), P(("loop", "group"), None), P(("loop", "group")))
    return jax.shard_map(
        on_device, mesh=mesh, in_specs=in_specs, out_specs=out_specs, check_vma=False
    )
```

profile of v0, /device:TPU:7, one launch (start us, length us, event | category | flops | bytes accessed | tf_op | source)
XLA Modules:
  0.0 738.9 jit_solution(17377193501999434338)
XLA Ops:
  7.2 0.0 copy-start
  7.2 0.0 all-reduce.6.cloned.1.call-start
  7.2 0.8 fusion.5
  8.1 0.8 fusion.12
  8.9 122.0 %all_gather.3 = bf16[256,1152]{1,0:T(8,128)(2,1)S(1)} all-gather(bf16[8,1152]{1,0:T(8,128)(2,1)S(1)} %fusion.12), channel_id=1, replica_groups=mesh['loop'=32,'group'=32] {'group'}, dimensions={0}, use_global_device_ids=true | all-gather | bytes 608256 | tf_op jit(solution)/shard_map/all_gather | solution.py:38
  130.9 21.9 %collective-permute-start = (bf16[256,1152]{1,0:T(8,128)(2,1)S(1)}, bf16[256,1152]{1,0:T(8,128)(2,1)S(1)}, u32[]{:S(2)}, u32[]{:S(2)}) collective-permute-start(bf16[256,1152]{1,0:T(8,128)(2,1)S(1)} %all_gather.3), channel_id=1, source_target_pairs={{0,32},{32,64},{64,96},{96,128},{128,160},{160,192},{192,224},{224... | collective-permute-start | bytes 1769480 | tf_op jit(solution)/shard_map/ppermute | solution.py:15
  154.1 0.8 fusion.4
  155.0 1.1 fusion.6
  156.1 16.5 %collective-permute-done = bf16[256,1152]{1,0:T(8,128)(2,1)S(1)} collective-permute-done((bf16[256,1152]{1,0:T(8,128)(2,1)S(1)}, bf16[256,1152]{1,0:T(8,128)(2,1)S(1)}, u32[]{:S(2)}, u32[]{:S(2)}) %collective-permute-start) | collective-permute-done | bytes 589856 | tf_op jit(solution)/shard_map/ppermute | solution.py:15
  172.6 15.3 %collective-permute-start.1 = (bf16[256,1152]{1,0:T(8,128)(2,1)S(1)}, bf16[256,1152]{1,0:T(8,128)(2,1)S(1)}, u32[]{:S(2)}, u32[]{:S(2)}) collective-permute-start(bf16[256,1152]{1,0:T(8,128)(2,1)S(1)} %collective-permute-done), channel_id=1, source_target_pairs={{0,32},{32,64},{64,96},{96,128},{128,160},{160,192},{192,224},{224... | collective-permute-start | bytes 1769480 | tf_op jit(solution)/shard_map/ppermute | solution.py:15
  187.9 0.0 copy-done
  187.9 1.5 fusion.13
  189.4 0.4 fusion.7
  189.8 1.5 fusion.9
  191.3 10.8 %collective-permute-done.1 = bf16[256,1152]{1,0:T(8,128)(2,1)S(1)} collective-permute-done((bf16[256,1152]{1,0:T(8,128)(2,1)S(1)}, bf16[256,1152]{1,0:T(8,128)(2,1)S(1)}, u32[]{:S(2)}, u32[]{:S(2)}) %collective-permute-start.1) | collective-permute-done | bytes 589856 | tf_op jit(solution)/shard_map/ppermute | solution.py:15
  202.1 0.4 fusion.8
  202.5 1.4 fusion.10
  203.9 0.0 all-reduce.6.cloned.1.call-update
  204.0 0.0 copy-start.1
  204.0 1.3 dynamic-slice
  205.9 0.2 fusion.14
  206.1 0.2 convolution_add_fusion.1
  206.3 0.3 multiply_reduce_fusion.1
  206.7 469.9 %all-reduce.6.cloned.1.call-done = (f32[256,1152]{1,0:T(8,128)}, f32[256,1152]{1,0:T(8,128)}, f32[256,1152]{1,0:T(8,128)}) async-done(((f32[256,1152]{1,0:T(8,128)}, f32[256,1152]{1,0:T(8,128)}, f32[256,1152]{1,0:T(8,128)}), (f32[256,1152]{1,0:T(8,128)}, f32[256,1152]{1,0:T(8,128)}, f32[256,1152]{1,0:T(8,128)})) %all-reduce.6.cloned.1.call-update) | async-done | bytes 3538960
  676.6 0.8 constant_dynamic-slice_fusion
  677.4 23.2 %collective-permute-start.2 = (f32[8,1152]{1,0:T(8,128)S(1)}, f32[8,1152]{1,0:T(8,128)S(1)}, u32[]{:S(2)}, u32[]{:S(2)}) collective-permute-start(f32[8,1152]{1,0:T(8,128)S(1)} %constant_dynamic-slice_fusion), channel_id=1, source_target_pairs={{0,992},{32,0},{64,32},{96,64},{128,96},{160,128},{192,160},{224,1... | collective-permute-start | bytes 110600 | tf_op jit(solution)/shard_map/ppermute | solution.py:15
  700.6 0.7 subtract_divide_fusion.1
  701.3 11.5 %collective-permute-done.2 = f32[8,1152]{1,0:T(8,128)S(1)} collective-permute-done((f32[8,1152]{1,0:T(8,128)S(1)}, f32[8,1152]{1,0:T(8,128)S(1)}, u32[]{:S(2)}, u32[]{:S(2)}) %collective-permute-start.2) | collective-permute-done | bytes 36896 | tf_op jit(solution)/shard_map/ppermute | solution.py:15
  712.8 0.8 dynamic-slice_add_fusion.1
  713.6 1.9 collective-permute-start.3
  715.5 0.5 add_add_fusion
  716.0 13.7 %collective-permute-done.3 = f32[8,1152]{1,0:T(8,128)S(1)} collective-permute-done((f32[8,1152]{1,0:T(8,128)S(1)}, f32[8,1152]{1,0:T(8,128)S(1)}, u32[]{:S(2)}, u32[]{:S(2)}) %collective-permute-start.3) | collective-permute-done | bytes 36896 | tf_op jit(solution)/shard_map/ppermute | solution.py:15
  729.7 0.0 copy-done.1
  729.7 1.0 multiply_reduce_fusion
  730.6 1.5 subtract_divide_fusion
  (3 shorter events, 0.0 us)
Async XLA Ops:
  7.2 180.7 %copy-start = (bf16[8,1152]{1,0:T(8,128)(2,1)S(1)}, bf16[8,1152]{1,0:T(8,128)(2,1)}, u32[]{:S(2)}) copy-start(bf16[8,1152]{1,0:T(8,128)(2,1)} %param.4) | copy-start | bytes 55300
  7.2 669.4 %all-reduce.6.cloned.1.call-start = ((), (), s32[]{:S(2)}) async-start(), calls=%async_computation | async-start | bytes 7077888
  130.9 41.7 %collective-permute-start = (bf16[256,1152]{1,0:T(8,128)(2,1)S(1)}, bf16[256,1152]{1,0:T(8,128)(2,1)S(1)}, u32[]{:S(2)}, u32[]{:S(2)}) collective-permute-start(bf16[256,1152]{1,0:T(8,128)(2,1)S(1)} %all_gather.3), channel_id=1, source_target_pairs={{0,32},{32,64},{64,96},{96,128},{128,160},{160,192},{192,224},{224... | collective-permute-start | bytes 1769480 | tf_op jit(solution)/shard_map/ppermute | solution.py:15
  172.6 29.5 %collective-permute-start.1 = (bf16[256,1152]{1,0:T(8,128)(2,1)S(1)}, bf16[256,1152]{1,0:T(8,128)(2,1)S(1)}, u32[]{:S(2)}, u32[]{:S(2)}) collective-permute-start(bf16[256,1152]{1,0:T(8,128)(2,1)S(1)} %collective-permute-done), channel_id=1, source_target_pairs={{0,32},{32,64},{64,96},{96,128},{128,160},{160,192},{192,224},{224... | collective-permute-start | bytes 1769480 | tf_op jit(solution)/shard_map/ppermute | solution.py:15
  204.0 525.7 %copy-start.1 = (bf16[8,1152]{1,0:T(8,128)(2,1)S(1)}, bf16[8,1152]{1,0:T(8,128)(2,1)}, u32[]{:S(2)}) copy-start(bf16[8,1152]{1,0:T(8,128)(2,1)} %param.5) | copy-start | bytes 55300
  677.4 35.4 %collective-permute-start.2 = (f32[8,1152]{1,0:T(8,128)S(1)}, f32[8,1152]{1,0:T(8,128)S(1)}, u32[]{:S(2)}, u32[]{:S(2)}) collective-permute-start(f32[8,1152]{1,0:T(8,128)S(1)} %constant_dynamic-slice_fusion), channel_id=1, source_target_pairs={{0,992},{32,0},{64,32},{96,64},{128,96},{160,128},{192,160},{224,1... | collective-permute-start | bytes 110600 | tf_op jit(solution)/shard_map/ppermute | solution.py:15
  713.6 16.1 %collective-permute-start.3 = (f32[8,1152]{1,0:T(8,128)S(1)}, f32[8,1152]{1,0:T(8,128)S(1)}, u32[]{:S(2)}, u32[]{:S(2)}) collective-permute-start(f32[8,1152]{1,0:T(8,128)S(1)} %dynamic-slice_add_fusion.1), channel_id=1, source_target_pairs={{0,992},{32,0},{64,32},{96,64},{128,96},{160,128},{192,160},{224,1... | collective-permute-start | bytes 110600 | tf_op jit(solution)/shard_map/ppermute | solution.py:15
Sparse Core Ops, SparseCore 0:
  204.1 472.4 all-reduce.5
where the time goes:
time: 740 us; the launch traced here: 739 us
  waiting for transfers between devices  522 us (71%)
  blocking collectives  122 us (16%)
  starting transfers between devices  62.4 us (8%)
  between operations  16.1 us (2%)
    unnamed x2, waiting for transfers between devices  470 us
    all_gather x1, blocking collectives, on_device(): block = lax.all_gather(txt_half, 'group', axis=0, tiled=True)  122 us
    ppermute x4, starting transfers between devices, passed_along(): return lax.ppermute(value, axis, pairs)  62.3 us
    ppermute x4, waiting for transfers between devices, passed_along(): return lax.ppermute(value, axis, pairs)  52.5 us
  transfers between devices with their start and end apart: 5, of which 5 were waited for; matrix products, arithmetic and copies ran while one was open for 1% of the time, Pallas kernels for 0%

commit v1 on v0

v1 whole, which is shorter than its diff:
```python
import jax
import jax.numpy as jnp
from jax import lax
from jax.experimental import pallas as pl
from jax.experimental.pallas import tpu as pltpu
from jax.sharding import Mesh, PartitionSpec as P

EPS = 1e-06
ROUNDS = 3
ROWS = 8
FAR, X, CORE, LINE, RING = 4, 4, 2, 8, 4
LOOP = ("far", "x", "core")
LANES = 128


def passed_along(value, steps):
    count = FAR * X * CORE
    return lax.ppermute(value, LOOP, [(s, (s + steps) % count) for s in range(count)])


def normalize(x):
    xf = x.astype(jnp.float32)
    norms = jnp.sqrt(jnp.sum(xf * xf, axis=-1, keepdims=True) + EPS)
    return xf / norms, norms


def project_back(grad, unit, norms):
    return (grad - unit * jnp.sum(unit * grad, axis=-1, keepdims=True)) / norms


def score_kernel(place_ref, param_ref, img_ref, txt_ref, gu_ref, gv_ref):
    scale, bias = param_ref[0], param_ref[1]
    img = normalize(img_ref[...])[0].astype(jnp.bfloat16)
    txt = normalize(txt_ref[...])[0].astype(jnp.bfloat16)
    dots = lax.dot_general(img, txt, (((1,), (1,)), ((), ())), preferred_element_type=jnp.float32)
    logit = scale * dots + bias
    row = lax.broadcasted_iota(jnp.int32, logit.shape, 0) - place_ref[0] * ROWS
    column = lax.broadcasted_iota(jnp.int32, logit.shape, 1) - place_ref[1] * (ROUNDS * ROWS)
    own = (row == column) & (row >= 0) & (row < ROWS)
    against = jnp.where(own, -logit, logit)
    decay = jnp.exp(-jnp.abs(against))
    loss = jnp.maximum(against, 0.0) + jnp.log1p(decay)
    chance = jnp.where(against >= 0, 1.0, decay) / (1.0 + decay)
    coef = jnp.where(own, -chance, chance) * scale
    width = img.shape[1]
    gu_ref[:, :width] = jnp.dot(
        coef.astype(jnp.bfloat16), txt, preferred_element_type=jnp.float32
    ).astype(jnp.bfloat16)
    gv_ref[...] = jnp.dot(
        coef.T.astype(jnp.bfloat16), img, preferred_element_type=jnp.float32
    ).astype(jnp.bfloat16)
    total = jnp.sum(loss, axis=1, keepdims=True)
    high = total.astype(jnp.bfloat16).astype(jnp.float32)
    lane = lax.broadcasted_iota(jnp.int32, (total.shape[0], LANES), 1)
    gu_ref[:, width:] = jnp.where(
        lane == 0, high, jnp.where(lane == 1, total - high, 0.0)
    ).astype(jnp.bfloat16)


def ring_sum_kernel(parts_ref, own_ref, back1_ref, back2_ref):
    parts = parts_ref[...].astype(jnp.float32)
    total = jnp.sum(parts.reshape(RING, ROUNDS * ROWS, parts.shape[1]), axis=0)
    own_ref[...] = total[:ROWS]
    back1_ref[...] = total[ROWS : 2 * ROWS]
    back2_ref[...] = total[2 * ROWS :]


def finish_kernel(parts_ref, img_ref, txt_ref, own_ref, back1_ref, back2_ref, ig_ref, tg_ref, loss_ref):
    width = img_ref.shape[1]
    parts = parts_ref[...].astype(jnp.float32)
    total = jnp.sum(parts.reshape(LINE, ROWS, parts.shape[1]), axis=0)
    ig_ref[...] = project_back(total[:, :width], *normalize(img_ref[...]))
    gv = own_ref[...] + back1_ref[...] + back2_ref[...]
    tg_ref[...] = project_back(gv, *normalize(txt_ref[...]))
    loss = jnp.sum(total[:, width:], axis=1, keepdims=True)
    row = lax.broadcasted_iota(jnp.int32, (ROWS, LANES), 0)
    lane = lax.broadcasted_iota(jnp.int32, (ROWS, LANES), 1)
    loss_ref[...] = jnp.sum(jnp.where(row == lane, loss, 0.0), axis=0, keepdims=True)


def on_device(images, texts, scale, bias):
    width = images.shape[1]
    place = jnp.stack([lax.axis_index("line"), lax.axis_index("ring")]).astype(jnp.int32)
    params = jnp.stack([scale, bias])
    before1 = passed_along(texts, 1)
    before2 = passed_along(texts, 2)
    line_imgs = lax.all_to_all(
        jnp.broadcast_to(images[None], (LINE, ROWS, width)), "line", 0, 0, tiled=True
    ).reshape(LINE * ROWS, width)
    visiting = jnp.concatenate([texts, before1, before2])
    visiting, line_imgs = lax.optimization_barrier((visiting, line_imgs))
    ring_txts = lax.all_to_all(
        jnp.broadcast_to(visiting[None], (RING, ROUNDS * ROWS, width)), "ring", 0, 0, tiled=True
    ).reshape(RING * ROUNDS * ROWS, width)
    smem = pl.BlockSpec(memory_space=pltpu.SMEM)
    vmem = pl.BlockSpec(memory_space=pltpu.VMEM)
    gu_parts, gv_parts = pl.pallas_call(
        score_kernel,
        out_shape=(
            jax.ShapeDtypeStruct((LINE * ROWS, width + LANES), jnp.bfloat16),
            jax.ShapeDtypeStruct((RING * ROUNDS * ROWS, width), jnp.bfloat16),
        ),
        in_specs=[smem, smem, vmem, vmem],
        out_specs=(vmem, vmem),
        name="score",
    )(place, params, line_imgs, ring_txts)
    gv_parts = lax.all_to_all(
        gv_parts.reshape(RING, ROUNDS * ROWS, width), "ring", 0, 0, tiled=True
    ).reshape(RING * ROUNDS * ROWS, width)
    piece = jax.ShapeDtypeStruct((ROWS, width), jnp.float32)
    own, back1, back2 = pl.pallas_call(
        ring_sum_kernel, out_shape=(piece,) * 3, in_specs=[vmem], out_specs=(vmem,) * 3, name="ring_sum"
    )(gv_parts)
    gu_parts, own = lax.optimization_barrier((gu_parts, own))
    back1 = passed_along(back1, -1)
    back2 = passed_along(back2, -2)
    gu_parts = lax.all_to_all(
        gu_parts.reshape(LINE, ROWS, width + LANES), "line", 0, 0, tiled=True
    ).reshape(LINE * ROWS, width + LANES)
    image_grad, text_grad, loss = pl.pallas_call(
        finish_kernel,
        out_shape=(piece, piece, jax.ShapeDtypeStruct((1, LANES), jnp.float32)),
        in_specs=[vmem] * 6,
        out_specs=(vmem,) * 3,
        name="finish",
    )(gu_parts, images, texts, own, back1, back2)
    return image_grad, text_grad, loss[0, :ROWS]


def solution(mesh):
    parts = Mesh(
        mesh.devices.reshape(FAR, X, CORE, LINE, RING), ("far", "x", "core", "line", "ring")
    )
    rows = P(("far", "x", "core", "line", "ring"), None)
    return jax.shard_map(
        on_device,
        mesh=parts,
        in_specs=(rows, rows, P(), P()),
        out_specs=(rows, rows, P(("far", "x", "core", "line", "ring"))),
        check_vma=False,
    )
```

time: 740 us -> 104 us (0.14)
  the two profiles are of different devices: /device:TPU:7 before, /device:TPU:135 now
where the time goes in v1:
time: 104 us; the launch traced here: 103 us
  starting transfers between devices  52.3 us (50%)
  waiting for transfers between devices  27.9 us (27%)
  blocking collectives  9.38 us (9%)
  Pallas kernels  5.71 us (5%)
  local copies, waits for them, and re-layouts  4.65 us (4%)
  between operations  2.02 us (2%)
  other arithmetic  1.24 us (1%)
    ppermute x4, starting transfers between devices, passed_along(): lax.ppermute(value, LOOP, [(s, (s + steps) % count) for s in range(count)])  27 us
    ppermute x4, waiting for transfers between devices, passed_along(): lax.ppermute(value, LOOP, [(s, (s + steps) % count) for s in range(count)])  23.8 us
    all_to_all x1, starting transfers between devices, on_device(): lax.all_to_all(jnp.broadcast_to(images[None], (LINE, ROWS, width)), 'line...  10.8 us
    all_to_all x1, starting transfers between devices, on_device(): lax.all_to_all(gu_parts.reshape(LINE, ROWS, width + LANES), 'line', 0, 0,...  10.3 us
    all_to_all x1, blocking collectives, on_device(): lax.all_to_all(gv_parts.reshape(RING, ROUNDS * ROWS, width), 'ring', 0, 0...  9.38 us
    all_to_all x1, starting transfers between devices, on_device(): lax.all_to_all(jnp.broadcast_to(visiting[None], (RING, ROUNDS * ROWS, wid...  4.18 us
    all_to_all x1, waiting for transfers between devices, on_device(): lax.all_to_all(jnp.broadcast_to(visiting[None], (RING, ROUNDS * ROWS, wid...  4.07 us
    pallas_call x1, Pallas kernels, on_device(): pl.pallas_call(score_kernel, out_shape=(jax.ShapeDtypeStruct((LINE * ROWS...  2.34 us
  transfers between devices with their start and end apart: 7, of which 3 were waited for; matrix products, arithmetic and copies ran while one was open for 1% of the time, Pallas kernels for 0%

profile of v1, /device:TPU:135, one launch (start us, length us, event | category | flops | bytes accessed | tf_op | source)
XLA Modules:
  0.0 103.2 jit_solution(8222805267849588719)
XLA Ops:
  0.6 1.4 %broadcast_in_dim.4 = bf16[8,8,1152]{2,1,0:T(8,128)(2,1)} broadcast(bf16[8,1152]{1,0:T(8,128)(2,1)} %img_ref.1), dimensions={1,2} | broadcast | bytes 165888 | tf_op jit(solution)/shard_map/broadcast_in_dim | solution.py:88
  2.0 0.0 copy-start.3
  2.0 10.8 %all-to-all-start = ((bf16[8,8,1152]{2,1,0:T(8,128)(2,1)}), bf16[8,8,1152]{2,1,0:T(8,128)(2,1)S(1)}, u32[]{:S(2)}, u32[]{:S(2)}) async-start(bf16[8,8,1152]{2,1,0:T(8,128)(2,1)} %broadcast_in_dim.4), calls=%async_computation | async-start | bytes 294912 | tf_op jit(solution)/shard_map/all_to_all | solution.py:87
  12.9 0.0 copy-done.3
  12.9 15.3 %collective-permute-start.1 = (bf16[8,1152]{1,0:T(8,128)(2,1)S(1)}, bf16[8,1152]{1,0:T(8,128)(2,1)S(1)}, u32[]{:S(2)}, u32[]{:S(2)}) collective-permute-start(bf16[8,1152]{1,0:T(8,128)(2,1)S(1)} %copy-done.3), channel_id=1, source_target_pairs={{0,64},{32,96},{64,128},{96,160},{128,192},{160,224},{192,256},{22... | collective-permute-start | bytes 55304 | tf_op jit(solution)/shard_map/ppermute | solution.py:18
  28.2 4.5 %collective-permute-start = (bf16[8,1152]{1,0:T(8,128)(2,1)S(1)}, bf16[8,1152]{1,0:T(8,128)(2,1)S(1)}, u32[]{:S(2)}, u32[]{:S(2)}) collective-permute-start(bf16[8,1152]{1,0:T(8,128)(2,1)S(1)} %copy-done.3), channel_id=1, source_target_pairs={{0,32},{32,64},{64,96},{96,128},{128,160},{160,192},{192,224},{224... | collective-permute-start | bytes 55304 | tf_op jit(solution)/shard_map/ppermute | solution.py:18
  34.0 0.0 collective-permute-done.1
  34.1 0.0 collective-permute-done
  34.1 0.0 all-to-all-done
  34.1 0.0 copy-start.2
  34.1 0.7 broadcast_in_dim.5
  34.8 0.0 copy-done.2
  34.8 4.2 %all-to-all-start.1 = ((bf16[4,24,1152]{2,1,0:T(8,128)(2,1)}), bf16[4,24,1152]{2,1,0:T(8,128)(2,1)S(1)}, u32[]{:S(2)}, u32[]{:S(2)}) async-start(bf16[4,24,1152]{2,1,0:T(8,128)(2,1)} %broadcast_in_dim.5), calls=%async_computation.1 | async-start | bytes 442368 | tf_op jit(solution)/shard_map/all_to_all | solution.py:92
  39.0 0.7 pad_maximum_fusion.1.param_ref
  39.7 0.6 pad_add_fusion.place_ref
  40.2 4.1 %all-to-all-done.1 = bf16[4,24,1152]{2,1,0:T(8,128)(2,1)S(1)} async-done(((bf16[4,24,1152]{2,1,0:T(8,128)(2,1)}), bf16[4,24,1152]{2,1,0:T(8,128)(2,1)S(1)}, u32[]{:S(2)}, u32[]{:S(2)}) %all-to-all-start.1) | async-done | bytes 221216 | tf_op jit(solution)/shard_map/all_to_all | solution.py:92
  44.3 0.0 copy-start
  44.3 0.7 copy-done
  45.0 2.3 %score.1 = (bf16[64,1280]{1,0:T(8,128)(2,1)}, bf16[96,1152]{1,0:T(8,128)(2,1)}) custom-call(s32[2]{0:T(128)} %pad_add_fusion.place_ref, f32[2]{0:T(128)} %pad_maximum_fusion.1.param_ref, bf16[64,1152]{1,0:T(8,128)(2,1)} %bitcast.17, bf16[96,1152]{1,0:T(8,128)(2,1)} %bitcast.15), custom_call_target="tpu_custom_call" | custom-call | tf_op jit(solution)/shard_map/score/pallas_call | solution.py:97
  47.3 9.4 %all_to_all.20 = bf16[4,24,1152]{2,1,0:T(8,128)(2,1)} all-to-all(bf16[4,24,1152]{2,1,0:T(8,128)(2,1)} %bitcast.18), channel_id=1, replica_groups=mesh['far'=4,'x'=4,'core'=2,'line'=8,'ring'=4] {'ring'}, dimensions={0} | all-to-all | bytes 442368 | tf_op jit(solution)/shard_map/all_to_all | solution.py:107
  56.7 1.6 %ring_sum.1 = (f32[8,1152]{1,0:T(8,128)}, f32[8,1152]{1,0:T(8,128)}, f32[8,1152]{1,0:T(8,128)}) custom-call(bf16[96,1152]{1,0:T(8,128)(2,1)} %bitcast.14), custom_call_target="tpu_custom_call" | custom-call | tf_op jit(solution)/shard_map/ring_sum/pallas_call | solution.py:111
  58.3 0.0 copy-start.7
  58.3 0.0 copy-start.6
  58.3 10.3 %all-to-all-start.3 = ((bf16[8,8,1280]{2,1,0:T(8,128)(2,1)}), bf16[8,8,1280]{2,1,0:T(8,128)(2,1)S(1)}, u32[]{:S(2)}, u32[]{:S(2)}) async-start(bf16[8,8,1280]{2,1,0:T(8,128)(2,1)} %bitcast.8), calls=%async_computation.3 | async-start | bytes 327680 | tf_op jit(solution)/shard_map/all_to_all | solution.py:117
  68.6 0.0 copy-done.7
  68.7 5.2 %collective-permute-start.2 = (f32[8,1152]{1,0:T(8,128)S(1)}, f32[8,1152]{1,0:T(8,128)S(1)}, u32[]{:S(2)}, u32[]{:S(2)}) collective-permute-start(f32[8,1152]{1,0:T(8,128)S(1)} %copy-done.7), channel_id=1, source_target_pairs={{0,992},{32,0},{64,32},{96,64},{128,96},{160,128},{192,160},{224,1... | collective-permute-start | bytes 110600 | tf_op jit(solution)/shard_map/ppermute | solution.py:18
  73.8 0.0 copy-done.6
  73.9 1.9 %collective-permute-start.3 = (f32[8,1152]{1,0:T(8,128)S(1)}, f32[8,1152]{1,0:T(8,128)S(1)}, u32[]{:S(2)}, u32[]{:S(2)}) collective-permute-start(f32[8,1152]{1,0:T(8,128)S(1)} %copy-done.6), channel_id=1, source_target_pairs={{0,960},{32,992},{64,0},{96,32},{128,64},{160,96},{192,128},{224,1... | collective-permute-start | bytes 110600 | tf_op jit(solution)/shard_map/ppermute | solution.py:18
  75.8 22.7 %collective-permute-done.2.back1_ref = f32[8,1152]{1,0:T(8,128)S(1)} collective-permute-done((f32[8,1152]{1,0:T(8,128)S(1)}, f32[8,1152]{1,0:T(8,128)S(1)}, u32[]{:S(2)}, u32[]{:S(2)}) %collective-permute-start.2) | collective-permute-done | bytes 36896 | tf_op jit(solution)/shard_map/ppermute | solution.py:18
  98.5 0.0 copy-start.4
  98.5 1.1 %collective-permute-done.3.back2_ref = f32[8,1152]{1,0:T(8,128)S(1)} collective-permute-done((f32[8,1152]{1,0:T(8,128)S(1)}, f32[8,1152]{1,0:T(8,128)S(1)}, u32[]{:S(2)}, u32[]{:S(2)}) %collective-permute-start.3) | collective-permute-done | bytes 36896 | tf_op jit(solution)/shard_map/ppermute | solution.py:18
  99.6 0.0 copy-start.5
  99.6 0.0 all-to-all-done.3
  99.6 0.0 copy-start.1
  99.6 0.0 copy-done.4
  99.6 0.6 copy-done.5
  100.2 0.1 copy-done.1
  100.3 1.8 %finish.1 = (f32[8,1152]{1,0:T(8,128)}, f32[8,1152]{1,0:T(8,128)}, f32[1,128]{1,0:T(1,128)}) custom-call(bf16[64,1280]{1,0:T(8,128)(2,1)} %bitcast.16, bf16[8,1152]{1,0:T(8,128)(2,1)} %img_ref.1, bf16[8,1152]{1,0:T(8,128)(2,1)} %txt_ref.1, f32[8,1152]{1,0:T(8,128)} %get-tuple-element.21.own_ref, f32[8,1152]{1,0:T(8,128)} %copy-done.4, f32[8,1152]{1,0:T(8,128)} %copy-done.5), custom_call_target="tpu_custom_call" | custom-call | tf_op jit(solution)/shard_map/finish/pallas_call | solution.py:120
  102.1 0.0 copy-start.8
  102.1 0.7 copy-done.8
  102.7 0.5 slice_bitcast_fusion
  (1 shorter events, 0.0 us)
Async XLA Ops:
  2.0 10.8 %copy-start.3 = (bf16[8,1152]{1,0:T(8,128)(2,1)S(1)}, bf16[8,1152]{1,0:T(8,128)(2,1)}, u32[]{:S(2)}) copy-start(bf16[8,1152]{1,0:T(8,128)(2,1)} %txt_ref.1) | copy-start | bytes 55300
  2.0 32.1 %all-to-all-start = ((bf16[8,8,1152]{2,1,0:T(8,128)(2,1)}), bf16[8,8,1152]{2,1,0:T(8,128)(2,1)S(1)}, u32[]{:S(2)}, u32[]{:S(2)}) async-start(bf16[8,8,1152]{2,1,0:T(8,128)(2,1)} %broadcast_in_dim.4), calls=%async_computation | async-start | bytes 294912 | tf_op jit(solution)/shard_map/all_to_all | solution.py:87
  12.9 21.2 %collective-permute-start.1 = (bf16[8,1152]{1,0:T(8,128)(2,1)S(1)}, bf16[8,1152]{1,0:T(8,128)(2,1)S(1)}, u32[]{:S(2)}, u32[]{:S(2)}) collective-permute-start(bf16[8,1152]{1,0:T(8,128)(2,1)S(1)} %copy-done.3), channel_id=1, source_target_pairs={{0,64},{32,96},{64,128},{96,160},{128,192},{160,224},{192,256},{22... | collective-permute-start | bytes 55304 | tf_op jit(solution)/shard_map/ppermute | solution.py:18
  28.2 5.8 %collective-permute-start = (bf16[8,1152]{1,0:T(8,128)(2,1)S(1)}, bf16[8,1152]{1,0:T(8,128)(2,1)S(1)}, u32[]{:S(2)}, u32[]{:S(2)}) collective-permute-start(bf16[8,1152]{1,0:T(8,128)(2,1)S(1)} %copy-done.3), channel_id=1, source_target_pairs={{0,32},{32,64},{64,96},{96,128},{128,160},{160,192},{192,224},{224... | collective-permute-start | bytes 55304 | tf_op jit(solution)/shard_map/ppermute | solution.py:18
  34.1 0.7 copy-start.2
  34.8 9.5 %all-to-all-start.1 = ((bf16[4,24,1152]{2,1,0:T(8,128)(2,1)}), bf16[4,24,1152]{2,1,0:T(8,128)(2,1)S(1)}, u32[]{:S(2)}, u32[]{:S(2)}) async-start(bf16[4,24,1152]{2,1,0:T(8,128)(2,1)} %broadcast_in_dim.5), calls=%async_computation.1 | async-start | bytes 442368 | tf_op jit(solution)/shard_map/all_to_all | solution.py:92
  44.3 0.7 copy-start
  58.3 10.3 %copy-start.7 = (f32[8,1152]{1,0:T(8,128)S(1)}, f32[8,1152]{1,0:T(8,128)}, u32[]{:S(2)}) copy-start(f32[8,1152]{1,0:T(8,128)} %get-tuple-element.22) | copy-start | bytes 110596
  58.3 15.5 %copy-start.6 = (f32[8,1152]{1,0:T(8,128)S(1)}, f32[8,1152]{1,0:T(8,128)}, u32[]{:S(2)}) copy-start(f32[8,1152]{1,0:T(8,128)} %get-tuple-element.23) | copy-start | bytes 110596
  58.3 41.3 %all-to-all-start.3 = ((bf16[8,8,1280]{2,1,0:T(8,128)(2,1)}), bf16[8,8,1280]{2,1,0:T(8,128)(2,1)S(1)}, u32[]{:S(2)}, u32[]{:S(2)}) async-start(bf16[8,8,1280]{2,1,0:T(8,128)(2,1)} %bitcast.8), calls=%async_computation.3 | async-start | bytes 327680 | tf_op jit(solution)/shard_map/all_to_all | solution.py:117
  68.7 29.8 %collective-permute-start.2 = (f32[8,1152]{1,0:T(8,128)S(1)}, f32[8,1152]{1,0:T(8,128)S(1)}, u32[]{:S(2)}, u32[]{:S(2)}) collective-permute-start(f32[8,1152]{1,0:T(8,128)S(1)} %copy-done.7), channel_id=1, source_target_pairs={{0,992},{32,0},{64,32},{96,64},{128,96},{160,128},{192,160},{224,1... | collective-permute-start | bytes 110600 | tf_op jit(solution)/shard_map/ppermute | solution.py:18
  73.9 25.7 %collective-permute-start.3 = (f32[8,1152]{1,0:T(8,128)S(1)}, f32[8,1152]{1,0:T(8,128)S(1)}, u32[]{:S(2)}, u32[]{:S(2)}) collective-permute-start(f32[8,1152]{1,0:T(8,128)S(1)} %copy-done.6), channel_id=1, source_target_pairs={{0,960},{32,992},{64,0},{96,32},{128,64},{160,96},{192,128},{224,1... | collective-permute-start | bytes 110600 | tf_op jit(solution)/shard_map/ppermute | solution.py:18
  98.5 1.1 %copy-start.4 = (f32[8,1152]{1,0:T(8,128)}, f32[8,1152]{1,0:T(8,128)S(1)}, u32[]{:S(2)}) copy-start(f32[8,1152]{1,0:T(8,128)S(1)} %collective-permute-done.2.back1_ref) | copy-start | bytes 110596
  99.6 0.6 copy-start.5
  99.6 0.7 copy-start.1
  102.1 0.7 copy-start.8

commit v2 on v1

v2 whole, which is shorter than its diff:
```python
import jax
import jax.numpy as jnp
from jax import lax
from jax.experimental import pallas as pl
from jax.experimental.pallas import tpu as pltpu
from jax.sharding import Mesh, PartitionSpec as P

EPS = 1e-06
ROUNDS = 3
ROWS = 8
AXES = ("far", "x", "core", "line", "ring")
FAR, X, CORE, LINE, RING = 4, 4, 2, 8, 4
CHIPS = ("far", "x")
NEAR = CORE * RING
LANES = 128
SMEM = pl.BlockSpec(memory_space=pltpu.SMEM)
VMEM = pl.BlockSpec(memory_space=pltpu.VMEM)


def next_chip(value, steps):
    count = FAR * X
    return lax.ppermute(value, CHIPS, [(s, (s + steps) % count) for s in range(count)])


def normalize(x):
    xf = x.astype(jnp.float32)
    norms = jnp.sqrt(jnp.sum(xf * xf, axis=-1, keepdims=True) + EPS)
    return xf / norms, norms


def project_back(grad, unit, norms):
    return (grad - unit * jnp.sum(unit * grad, axis=-1, keepdims=True)) / norms


def spread_kernel(img_ref, out_ref):
    img = img_ref[...].astype(jnp.float32)
    out_ref[...] = jnp.concatenate([img] * LINE).astype(out_ref.dtype)


def pair_kernel(own_ref, before_ref, out_ref):
    pair = [own_ref[...].astype(jnp.float32), before_ref[...].astype(jnp.float32)]
    out_ref[...] = jnp.concatenate(pair * NEAR).astype(out_ref.dtype)


def score_kernel(scale_ref, bias_ref, img_ref, txt_ref, gu_ref, gv_ref):
    scale, bias = scale_ref[0], bias_ref[0]
    core, line, ring = lax.axis_index("core"), lax.axis_index("line"), lax.axis_index("ring")
    img = normalize(img_ref[...])[0].astype(jnp.bfloat16)
    txt = normalize(txt_ref[...])[0].astype(jnp.bfloat16)
    dots = lax.dot_general(img, txt, (((1,), (1,)), ((), ())), preferred_element_type=jnp.float32)
    logit = scale * dots + bias
    row = lax.broadcasted_iota(jnp.int32, logit.shape, 0)
    column = lax.broadcasted_iota(jnp.int32, logit.shape, 1)
    back = core - column // (RING * 2 * ROWS) + 2 * (column // ROWS % 2)
    scored = (back >= 0) & (back < ROUNDS)
    row = row - line * ROWS
    own = (row >= 0) & (row < ROWS) & (column == (core * RING + ring) * (2 * ROWS) + row)
    against = jnp.where(own, -logit, logit)
    decay = jnp.exp(-jnp.abs(against))
    loss = jnp.where(scored, jnp.maximum(against, 0.0) + jnp.log1p(decay), 0.0)
    chance = jnp.where(against >= 0, 1.0, decay) / (1.0 + decay)
    coef = jnp.where(scored, jnp.where(own, -chance, chance) * scale, 0.0)
    width = img.shape[1]
    gv_ref[...] = jnp.dot(
        coef.T.astype(jnp.bfloat16), img, preferred_element_type=jnp.float32
    ).astype(jnp.bfloat16)
    gu_ref[:, :width] = jnp.dot(
        coef.astype(jnp.bfloat16), txt, preferred_element_type=jnp.float32
    ).astype(jnp.bfloat16)
    total = jnp.sum(loss, axis=1, keepdims=True)
    high = total.astype(jnp.bfloat16).astype(jnp.float32)
    lane = lax.broadcasted_iota(jnp.int32, (total.shape[0], LANES), 1)
    gu_ref[:, width:] = jnp.where(
        lane == 0, high, jnp.where(lane == 1, total - high, 0.0)
    ).astype(jnp.bfloat16)


def near_sum_kernel(parts_ref, own_ref, back_ref):
    parts = parts_ref[...].astype(jnp.float32)
    total = jnp.sum(parts.reshape(NEAR, 2 * ROWS, parts.shape[1]), axis=0)
    own_ref[...] = total[:ROWS]
    back_ref[...] = total[ROWS:].astype(back_ref.dtype)


def finish_kernel(parts_ref, img_ref, txt_ref, own_ref, back_ref, ig_ref, tg_ref, loss_ref):
    width = img_ref.shape[1]
    parts = parts_ref[...].astype(jnp.float32)
    total = jnp.sum(parts.reshape(LINE, ROWS, parts.shape[1]), axis=0)
    ig_ref[...] = project_back(total[:, :width], *normalize(img_ref[...]))
    gv = own_ref[...] + back_ref[...].astype(jnp.float32)
    tg_ref[...] = project_back(gv, *normalize(txt_ref[...]))
    loss = jnp.sum(total[:, width:], axis=1, keepdims=True)
    row = lax.broadcasted_iota(jnp.int32, (ROWS, ROWS), 0)
    lane = lax.broadcasted_iota(jnp.int32, (ROWS, ROWS), 1)
    loss_ref[...] = jnp.sum(jnp.where(row == lane, loss, 0.0), axis=0)


def on_device(images, texts, scale, bias):
    width = images.shape[1]
    half, full = jnp.bfloat16, jnp.float32

    def shape(rows, columns, kind):
        return jax.ShapeDtypeStruct((rows, columns), kind)

    def exchange(value, axes, peers):
        pieces = value.reshape(peers, value.shape[0] // peers, value.shape[1])
        return lax.all_to_all(pieces, axes, 0, 0, tiled=True).reshape(value.shape)

    before = next_chip(texts, 1)
    spread = pl.pallas_call(
        spread_kernel,
        out_shape=shape(LINE * ROWS, width, half),
        in_specs=[VMEM],
        out_specs=VMEM,
        cost_estimate=pl.CostEstimate(flops=10**10, bytes_accessed=10**6, transcendentals=0),
        name="spread",
    )(images)
    line_imgs = exchange(spread, "line", LINE)
    pairs = pl.pallas_call(
        pair_kernel,
        out_shape=shape(NEAR * 2 * ROWS, width, half),
        in_specs=[VMEM, VMEM],
        out_specs=VMEM,
        name="pair",
    )(texts, before)
    near_txts = exchange(pairs, ("core", "ring"), NEAR)
    gu_parts, gv_parts = pl.pallas_call(
        score_kernel,
        out_shape=(shape(LINE * ROWS, width + LANES, half), shape(NEAR * 2 * ROWS, width, half)),
        in_specs=[SMEM, SMEM, VMEM, VMEM],
        out_specs=(VMEM, VMEM),
        name="score",
    )(scale.reshape(1), bias.reshape(1), line_imgs, near_txts)
    gv_parts = exchange(gv_parts, ("core", "ring"), NEAR)
    gu_parts = exchange(gu_parts, "line", LINE)
    own, back = pl.pallas_call(
        near_sum_kernel,
        out_shape=(shape(ROWS, width, full), shape(ROWS, width, half)),
        in_specs=[VMEM],
        out_specs=(VMEM, VMEM),
        name="near_sum",
    )(gv_parts)
    back = next_chip(back, -1)
    return pl.pallas_call(
        finish_kernel,
        out_shape=(
            shape(ROWS, width, full),
            shape(ROWS, width, full),
            jax.ShapeDtypeStruct((ROWS,), full),
        ),
        in_specs=[VMEM] * 5,
        out_specs=(VMEM, VMEM, VMEM),
        name="finish",
    )(gu_parts, images, texts, own, back)


def solution(mesh):
    parts = Mesh(mesh.devices.reshape(FAR, X, CORE, LINE, RING), AXES)
    rows = P(AXES, None)
    return jax.shard_map(
        on_device,
        mesh=parts,
        in_specs=(rows, rows, P(), P()),
        out_specs=(rows, rows, P(AXES)),
        check_vma=False,
    )
```

time: 104 us -> 102 us (0.981)
  the two profiles are of different devices: /device:TPU:135 before, /device:TPU:134 now
where the time goes in v2:
time: 102 us
  starting transfers between devices  43.4 us (43%)
  waiting for transfers between devices  33.9 us (33%)
  blocking collectives  11.8 us (12%)
  Pallas kernels  8.82 us (9%)
  between operations  1.96 us (2%)
  local copies, waits for them, and re-layouts  1.94 us (2%)
    all_to_all x3, starting transfers between devices, exchange(): return lax.all_to_all(pieces, axes, 0, 0, tiled=True).reshape(value.shape)  25.8 us
    ppermute x2, waiting for transfers between devices, next_chip(): lax.ppermute(value, CHIPS, [(s, (s + steps) % count) for s in range(count)])  22.1 us
    ppermute x2, starting transfers between devices, next_chip(): lax.ppermute(value, CHIPS, [(s, (s + steps) % count) for s in range(count)])  17.5 us
    all_to_all x1, blocking collectives, exchange(): return lax.all_to_all(pieces, axes, 0, 0, tiled=True).reshape(value.shape)  11.8 us
    all_to_all x3, waiting for transfers between devices, exchange(): return lax.all_to_all(pieces, axes, 0, 0, tiled=True).reshape(value.shape)  11.7 us
    pallas_call x1, Pallas kernels, on_device(): pl.pallas_call(score_kernel, out_shape=(shape(LINE * ROWS, width + LANES,...  2.57 us
  transfers between devices with their start and end apart: 5, of which 4 were waited for; matrix products, arithmetic and copies ran while one was open for 0% of the time, Pallas kernels for 3%

profile of v2, /device:TPU:134, one launch (start us, length us, event | category | flops | bytes accessed | tf_op | source)
XLA Modules:
  0.0 101.7 jit_solution(2401582719299923146)
XLA Ops:
  0.6 15.6 %collective-permute-start = (bf16[8,1152]{1,0:T(8,128)(2,1)}, bf16[8,1152]{1,0:T(8,128)(2,1)S(1)}, u32[]{:S(2)}, u32[]{:S(2)}) collective-permute-start(bf16[8,1152]{1,0:T(8,128)(2,1)} %txt_ref.1), channel_id=1, source_target_pairs={{0,64},{64,128},{128,192},{192,256},{256,320},{320,384},{384,448},... | collective-permute-start | bytes 55304 | tf_op jit(solution)/shard_map/ppermute | solution.py:22
  16.3 1.7 %collective-permute-done.before_ref = bf16[8,1152]{1,0:T(8,128)(2,1)S(1)} collective-permute-done((bf16[8,1152]{1,0:T(8,128)(2,1)}, bf16[8,1152]{1,0:T(8,128)(2,1)S(1)}, u32[]{:S(2)}, u32[]{:S(2)}) %collective-permute-start) | collective-permute-done | bytes 18464 | tf_op jit(solution)/shard_map/ppermute | solution.py:22
  17.9 0.0 copy-start.4
  17.9 0.6 copy-done.4
  18.5 1.5 %pair.1 = bf16[128,1152]{1,0:T(8,128)(2,1)} custom-call(bf16[8,1152]{1,0:T(8,128)(2,1)} %txt_ref.1, bf16[8,1152]{1,0:T(8,128)(2,1)} %copy-done.4), custom_call_target="tpu_custom_call" | custom-call | tf_op jit(solution)/shard_map/pair/pallas_call | solution.py:119
  20.0 4.5 %all-to-all-start.1 = ((bf16[8,16,1152]{2,1,0:T(8,128)(2,1)}), bf16[8,16,1152]{2,1,0:T(8,128)(2,1)S(1)}, u32[]{:S(2)}, u32[]{:S(2)}) async-start(bf16[8,16,1152]{2,1,0:T(8,128)(2,1)} %bitcast.14), calls=%async_computation.1 | async-start | bytes 589824 | tf_op jit(solution)/shard_map/all_to_all | solution.py:107
  24.5 1.4 %spread.1 = bf16[64,1152]{1,0:T(8,128)(2,1)} custom-call(bf16[8,1152]{1,0:T(8,128)(2,1)} %img_ref.3), custom_call_target="tpu_custom_call" | custom-call | flops 10000000000 | bytes 1000000 | tf_op jit(solution)/shard_map/spread/pallas_call | solution.py:110
  25.9 5.9 %all-to-all-done.1 = bf16[8,16,1152]{2,1,0:T(8,128)(2,1)S(1)} async-done(((bf16[8,16,1152]{2,1,0:T(8,128)(2,1)}), bf16[8,16,1152]{2,1,0:T(8,128)(2,1)S(1)}, u32[]{:S(2)}, u32[]{:S(2)}) %all-to-all-start.1) | async-done | bytes 294944 | tf_op jit(solution)/shard_map/all_to_all | solution.py:107
  31.7 0.0 copy-start
  31.7 11.3 %all-to-all-start = ((bf16[8,8,1152]{2,1,0:T(8,128)(2,1)}), bf16[8,8,1152]{2,1,0:T(8,128)(2,1)S(1)}, u32[]{:S(2)}, u32[]{:S(2)}) async-start(bf16[8,8,1152]{2,1,0:T(8,128)(2,1)} %bitcast.18), calls=%async_computation | async-start | bytes 294912 | tf_op jit(solution)/shard_map/all_to_all | solution.py:107
  44.3 5.9 %all-to-all-done = bf16[8,8,1152]{2,1,0:T(8,128)(2,1)S(1)} async-done(((bf16[8,8,1152]{2,1,0:T(8,128)(2,1)}), bf16[8,8,1152]{2,1,0:T(8,128)(2,1)S(1)}, u32[]{:S(2)}, u32[]{:S(2)}) %all-to-all-start) | async-done | bytes 147488 | tf_op jit(solution)/shard_map/all_to_all | solution.py:107
  50.2 0.0 copy-start.2
  50.2 0.0 copy-done
  50.2 0.7 copy-done.2
  50.8 2.6 %score.1 = (bf16[64,1280]{1,0:T(8,128)(2,1)}, bf16[128,1152]{1,0:T(8,128)(2,1)}) custom-call(f32[1]{0:T(128)} %bitcast.10.scale_ref, f32[1]{0:T(128)} %bitcast.11.bias_ref, bf16[64,1152]{1,0:T(8,128)(2,1)} %bitcast.16, bf16[128,1152]{1,0:T(8,128)(2,1)} %bitcast.12), custom_call_target="tpu_custom_call" | custom-call | tf_op jit(solution)/shard_map/score/pallas_call | solution.py:127
  53.4 11.8 %all_to_all.20 = bf16[8,16,1152]{2,1,0:T(8,128)(2,1)} all-to-all(bf16[8,16,1152]{2,1,0:T(8,128)(2,1)} %bitcast.17), channel_id=1, replica_groups=mesh['far'=4,'x'=4,'core'=2,'line'=8,'ring'=4] {'core','ring'}, dimensions={0} | all-to-all | bytes 589824 | tf_op jit(solution)/shard_map/all_to_all | solution.py:107
  65.2 10.1 %all-to-all-start.2 = ((bf16[8,8,1280]{2,1,0:T(8,128)(2,1)}), bf16[8,8,1280]{2,1,0:T(8,128)(2,1)S(1)}, u32[]{:S(2)}, u32[]{:S(2)}) async-start(bf16[8,8,1280]{2,1,0:T(8,128)(2,1)} %bitcast.6), calls=%async_computation.2 | async-start | bytes 327680 | tf_op jit(solution)/shard_map/all_to_all | solution.py:107
  75.3 1.6 %near_sum.1 = (f32[8,1152]{1,0:T(8,128)}, bf16[8,1152]{1,0:T(8,128)(2,1)}) custom-call(bf16[128,1152]{1,0:T(8,128)(2,1)} %bitcast.13), custom_call_target="tpu_custom_call" | custom-call | tf_op jit(solution)/shard_map/near_sum/pallas_call | solution.py:136
  76.9 1.9 %collective-permute-start.1 = (bf16[8,1152]{1,0:T(8,128)(2,1)}, bf16[8,1152]{1,0:T(8,128)(2,1)S(1)}, u32[]{:S(2)}, u32[]{:S(2)}) collective-permute-start(bf16[8,1152]{1,0:T(8,128)(2,1)} %get-tuple-element.10), channel_id=1, source_target_pairs={{0,960},{64,0},{128,64},{192,128},{256,192},{320,256},{384,320},{4... | collective-permute-start | bytes 55304 | tf_op jit(solution)/shard_map/ppermute | solution.py:22
  78.8 20.5 %collective-permute-done.1.back_ref = bf16[8,1152]{1,0:T(8,128)(2,1)S(1)} collective-permute-done((bf16[8,1152]{1,0:T(8,128)(2,1)}, bf16[8,1152]{1,0:T(8,128)(2,1)S(1)}, u32[]{:S(2)}, u32[]{:S(2)}) %collective-permute-start.1) | collective-permute-done | bytes 18464 | tf_op jit(solution)/shard_map/ppermute | solution.py:22
  99.3 0.0 copy-start.3
  99.3 0.0 all-to-all-done.2
  99.3 0.0 copy-start.1
  99.3 0.6 copy-done.3
  99.9 0.1 copy-done.1
  99.9 1.8 %finish.1 = (f32[8,1152]{1,0:T(8,128)}, f32[8,1152]{1,0:T(8,128)}, f32[8]{0:T(128)}) custom-call(bf16[64,1280]{1,0:T(8,128)(2,1)} %bitcast.15, bf16[8,1152]{1,0:T(8,128)(2,1)} %img_ref.3, bf16[8,1152]{1,0:T(8,128)(2,1)} %txt_ref.1, f32[8,1152]{1,0:T(8,128)} %get-tuple-element.9.own_ref, bf16[8,1152]{1,0:T(8,128)(2,1)} %copy-done.3), custom_call_target="tpu_custom_call" | custom-call | tf_op jit(solution)/shard_map/finish/pallas_call | solution.py:144
Async XLA Ops:
  0.6 17.3 %collective-permute-start = (bf16[8,1152]{1,0:T(8,128)(2,1)}, bf16[8,1152]{1,0:T(8,128)(2,1)S(1)}, u32[]{:S(2)}, u32[]{:S(2)}) collective-permute-start(bf16[8,1152]{1,0:T(8,128)(2,1)} %txt_ref.1), channel_id=1, source_target_pairs={{0,64},{64,128},{128,192},{192,256},{256,320},{320,384},{384,448},... | collective-permute-start | bytes 55304 | tf_op jit(solution)/shard_map/ppermute | solution.py:22
  17.9 0.6 copy-start.4
  20.0 11.7 %all-to-all-start.1 = ((bf16[8,16,1152]{2,1,0:T(8,128)(2,1)}), bf16[8,16,1152]{2,1,0:T(8,128)(2,1)S(1)}, u32[]{:S(2)}, u32[]{:S(2)}) async-start(bf16[8,16,1152]{2,1,0:T(8,128)(2,1)} %bitcast.14), calls=%async_computation.1 | async-start | bytes 589824 | tf_op jit(solution)/shard_map/all_to_all | solution.py:107
  31.7 18.4 %copy-start = (bf16[8,16,1152]{2,1,0:T(8,128)(2,1)}, bf16[8,16,1152]{2,1,0:T(8,128)(2,1)S(1)}, u32[]{:S(2)}) copy-start(bf16[8,16,1152]{2,1,0:T(8,128)(2,1)S(1)} %all-to-all-done.1) | copy-start | bytes 884740
  31.7 18.4 %all-to-all-start = ((bf16[8,8,1152]{2,1,0:T(8,128)(2,1)}), bf16[8,8,1152]{2,1,0:T(8,128)(2,1)S(1)}, u32[]{:S(2)}, u32[]{:S(2)}) async-start(bf16[8,8,1152]{2,1,0:T(8,128)(2,1)} %bitcast.18), calls=%async_computation | async-start | bytes 294912 | tf_op jit(solution)/shard_map/all_to_all | solution.py:107
  50.2 0.7 copy-start.2
  65.2 34.1 %all-to-all-start.2 = ((bf16[8,8,1280]{2,1,0:T(8,128)(2,1)}), bf16[8,8,1280]{2,1,0:T(8,128)(2,1)S(1)}, u32[]{:S(2)}, u32[]{:S(2)}) async-start(bf16[8,8,1280]{2,1,0:T(8,128)(2,1)} %bitcast.6), calls=%async_computation.2 | async-start | bytes 327680 | tf_op jit(solution)/shard_map/all_to_all | solution.py:107
  76.9 22.4 %collective-permute-start.1 = (bf16[8,1152]{1,0:T(8,128)(2,1)}, bf16[8,1152]{1,0:T(8,128)(2,1)S(1)}, u32[]{:S(2)}, u32[]{:S(2)}) collective-permute-start(bf16[8,1152]{1,0:T(8,128)(2,1)} %get-tuple-element.10), channel_id=1, source_target_pairs={{0,960},{64,0},{128,64},{192,128},{256,192},{320,256},{384,320},{4... | collective-permute-start | bytes 55304 | tf_op jit(solution)/shard_map/ppermute | solution.py:22
  99.3 0.6 copy-start.3
  99.3 0.7 copy-start.1

commit v3 on v2

--- a/solution.py
+++ b/solution.py
@@ -15,6 +15,7 @@
 LANES = 128
 SMEM = pl.BlockSpec(memory_space=pltpu.SMEM)
 VMEM = pl.BlockSpec(memory_space=pltpu.VMEM)
+ROOM = pltpu.CompilerParams(vmem_limit_bytes=8 * 2**20)
 
 
 def next_chip(value, steps):
@@ -112,7 +113,8 @@
         out_shape=shape(LINE * ROWS, width, half),
         in_specs=[VMEM],
         out_specs=VMEM,
-        cost_estimate=pl.CostEstimate(flops=10**10, bytes_accessed=10**6, transcendentals=0),
+        cost_estimate=pl.CostEstimate(flops=10**8, bytes_accessed=10**5, transcendentals=0),
+        compiler_params=ROOM,
         name="spread",
     )(images)
     line_imgs = exchange(spread, "line", LINE)
@@ -121,14 +123,18 @@
         out_shape=shape(NEAR * 2 * ROWS, width, half),
         in_specs=[VMEM, VMEM],
         out_specs=VMEM,
+        compiler_params=ROOM,
+        cost_estimate=pl.CostEstimate(flops=2*10**10, bytes_accessed=10**6, transcendentals=0),
         name="pair",
     )(texts, before)
+    pairs, line_imgs = lax.optimization_barrier((pairs, line_imgs))
     near_txts = exchange(pairs, ("core", "ring"), NEAR)
     gu_parts, gv_parts = pl.pallas_call(
         score_kernel,
         out_shape=(shape(LINE * ROWS, width + LANES, half), shape(NEAR * 2 * ROWS, width, half)),
         in_specs=[SMEM, SMEM, VMEM, VMEM],
         out_specs=(VMEM, VMEM),
+        compiler_params=ROOM,
         name="score",
     )(scale.reshape(1), bias.reshape(1), line_imgs, near_txts)
     gv_parts = exchange(gv_parts, ("core", "ring"), NEAR)
@@ -138,6 +144,7 @@
         out_shape=(shape(ROWS, width, full), shape(ROWS, width, half)),
         in_specs=[VMEM],
         out_specs=(VMEM, VMEM),
+        compiler_params=ROOM,
         name="near_sum",
     )(gv_parts)
     back = next_chip(back, -1)
@@ -150,6 +157,7 @@
         ),
         in_specs=[VMEM] * 5,
         out_specs=(VMEM, VMEM, VMEM),
+        compiler_params=ROOM,
         name="finish",
     )(gu_parts, images, texts, own, back)
 

time: 102 us -> 89.1 us (0.87)
  the two profiles are of different devices: /device:TPU:134 before, /device:TPU:6 now
where the time goes in v3:
time: 89.1 us; the launch traced here: 88.5 us
  starting transfers between devices  39.2 us (44%)
  waiting for transfers between devices  32.1 us (36%)
  blocking collectives  10.8 us (12%)
  Pallas kernels  3.74 us (4%)
  between operations  1.97 us (2%)
    all_to_all x3, starting transfers between devices, exchange(): return lax.all_to_all(pieces, axes, 0, 0, tiled=True).reshape(value.shape)  21.6 us
    ppermute x2, starting transfers between devices, next_chip(): lax.ppermute(value, CHIPS, [(s, (s + steps) % count) for s in range(count)])  17.6 us
    all_to_all x3, waiting for transfers between devices, exchange(): return lax.all_to_all(pieces, axes, 0, 0, tiled=True).reshape(value.shape)  17.3 us
    ppermute x2, waiting for transfers between devices, next_chip(): lax.ppermute(value, CHIPS, [(s, (s + steps) % count) for s in range(count)])  14.7 us
    all_to_all x1, blocking collectives, exchange(): return lax.all_to_all(pieces, axes, 0, 0, tiled=True).reshape(value.shape)  10.8 us
  transfers between devices with their start and end apart: 5, of which 3 were waited for; matrix products, arithmetic and copies ran while one was open for 0% of the time, Pallas kernels for 2%

profile of v3, /device:TPU:6, one launch (start us, length us, event | category | flops | bytes accessed | tf_op | source)
XLA Modules:
  0.0 88.5 jit_solution(14118992668929103309)
XLA Ops:
  0.6 15.6 %collective-permute-start = (bf16[8,1152]{1,0:T(8,128)(2,1)}, bf16[8,1152]{1,0:T(8,128)(2,1)S(1)}, u32[]{:S(2)}, u32[]{:S(2)}) collective-permute-start(bf16[8,1152]{1,0:T(8,128)(2,1)} %txt_ref.1), channel_id=1, source_target_pairs={{0,64},{64,128},{128,192},{192,256},{256,320},{320,384},{384,448},... | collective-permute-start | bytes 55304 | tf_op jit(solution)/shard_map/ppermute | solution.py:23
  16.3 0.0 copy-start
  16.3 0.7 copy-done
  17.0 0.7 spread.1
  17.7 0.0 copy-start.2
  17.7 12.7 %all-to-all-start = ((bf16[8,8,1152]{2,1,0:T(8,128)(2,1)}), bf16[8,8,1152]{2,1,0:T(8,128)(2,1)S(1)}, u32[]{:S(2)}, u32[]{:S(2)}) async-start(bf16[8,8,1152]{2,1,0:T(8,128)(2,1)} %bitcast.2), calls=%async_computation | async-start | bytes 294912 | tf_op jit(solution)/shard_map/all_to_all | solution.py:108
  30.3 0.0 collective-permute-done.before_ref
  30.3 0.0 copy-done.2
  30.3 0.7 pair.1
  31.1 11.4 %all-to-all-done = bf16[8,8,1152]{2,1,0:T(8,128)(2,1)S(1)} async-done(((bf16[8,8,1152]{2,1,0:T(8,128)(2,1)}), bf16[8,8,1152]{2,1,0:T(8,128)(2,1)S(1)}, u32[]{:S(2)}, u32[]{:S(2)}) %all-to-all-start) | async-done | bytes 147488 | tf_op jit(solution)/shard_map/all_to_all | solution.py:108
  42.5 4.5 %all-to-all-start.1 = ((bf16[8,16,1152]{2,1,0:T(8,128)(2,1)}), bf16[8,16,1152]{2,1,0:T(8,128)(2,1)S(1)}, u32[]{:S(2)}, u32[]{:S(2)}) async-start(bf16[8,16,1152]{2,1,0:T(8,128)(2,1)} %bitcast.4), calls=%async_computation.1 | async-start | bytes 589824 | tf_op jit(solution)/shard_map/all_to_all | solution.py:108
  48.2 6.0 %all-to-all-done.1 = bf16[8,16,1152]{2,1,0:T(8,128)(2,1)S(1)} async-done(((bf16[8,16,1152]{2,1,0:T(8,128)(2,1)}), bf16[8,16,1152]{2,1,0:T(8,128)(2,1)S(1)}, u32[]{:S(2)}, u32[]{:S(2)}) %all-to-all-start.1) | async-done | bytes 294944 | tf_op jit(solution)/shard_map/all_to_all | solution.py:108
  54.2 1.5 %score.1 = (bf16[64,1280]{1,0:T(8,128)(2,1)}, bf16[128,1152]{1,0:T(8,128)(2,1)S(1)}) custom-call(f32[1]{0:T(128)} %bitcast.10.scale_ref, f32[1]{0:T(128)} %bitcast.11.bias_ref, bf16[64,1152]{1,0:T(8,128)(2,1)S(1)} %bitcast.15, bf16[128,1152]{1,0:T(8,128)(2,1)S(1)} %bitcast.12), custom_call_target="tpu_custom_call" | custom-call | tf_op jit(solution)/shard_map/score/pallas_call | solution.py:132
  55.6 0.0 copy-start.1
  55.7 10.8 %all_to_all.20 = bf16[8,16,1152]{2,1,0:T(8,128)(2,1)S(1)} all-to-all(bf16[8,16,1152]{2,1,0:T(8,128)(2,1)S(1)} %bitcast.16), channel_id=1, replica_groups=mesh['far'=4,'x'=4,'core'=2,'line'=8,'ring'=4] {'core','ring'}, dimensions={0} | all-to-all | bytes 589824 | tf_op jit(solution)/shard_map/all_to_all | solution.py:108
  66.4 4.5 %all-to-all-start.2 = ((bf16[8,8,1280]{2,1,0:T(8,128)(2,1)}), bf16[8,8,1280]{2,1,0:T(8,128)(2,1)S(1)}, u32[]{:S(2)}, u32[]{:S(2)}) async-start(bf16[8,8,1280]{2,1,0:T(8,128)(2,1)} %bitcast.6), calls=%async_computation.2 | async-start | bytes 327680 | tf_op jit(solution)/shard_map/all_to_all | solution.py:108
  71.0 1.9 %collective-permute-start.1 = (bf16[8,1152]{1,0:T(8,128)(2,1)S(1)}, bf16[8,1152]{1,0:T(8,128)(2,1)S(1)}, u32[]{:S(2)}, u32[]{:S(2)}) collective-permute-start(bf16[8,1152]{1,0:T(8,128)(2,1)S(1)} %get-tuple-element.14), channel_id=1, source_target_pairs={{0,960},{64,0},{128,64},{192,128},{256,192},{320,256},{384,320},{4... | collective-permute-start | bytes 55304 | tf_op jit(solution)/shard_map/ppermute | solution.py:23
  72.9 14.7 %collective-permute-done.1.back_ref = bf16[8,1152]{1,0:T(8,128)(2,1)S(1)} collective-permute-done((bf16[8,1152]{1,0:T(8,128)(2,1)S(1)}, bf16[8,1152]{1,0:T(8,128)(2,1)S(1)}, u32[]{:S(2)}, u32[]{:S(2)}) %collective-permute-start.1) | collective-permute-done | bytes 18464 | tf_op jit(solution)/shard_map/ppermute | solution.py:23
  87.6 0.0 all-to-all-done.2
  87.6 0.0 copy-done.1
  87.6 0.8 finish.1
  (1 shorter events, 0.0 us)
Async XLA Ops:
  0.6 29.7 %collective-permute-start = (bf16[8,1152]{1,0:T(8,128)(2,1)}, bf16[8,1152]{1,0:T(8,128)(2,1)S(1)}, u32[]{:S(2)}, u32[]{:S(2)}) collective-permute-start(bf16[8,1152]{1,0:T(8,128)(2,1)} %txt_ref.1), channel_id=1, source_target_pairs={{0,64},{64,128},{128,192},{192,256},{256,320},{320,384},{384,448},... | collective-permute-start | bytes 55304 | tf_op jit(solution)/shard_map/ppermute | solution.py:23
  16.3 0.7 copy-start
  17.7 12.7 %copy-start.2 = (bf16[8,1152]{1,0:T(8,128)(2,1)S(1)}, bf16[8,1152]{1,0:T(8,128)(2,1)}, u32[]{:S(2)}) copy-start(bf16[8,1152]{1,0:T(8,128)(2,1)} %txt_ref.1) | copy-start | bytes 55300
  17.7 24.8 %all-to-all-start = ((bf16[8,8,1152]{2,1,0:T(8,128)(2,1)}), bf16[8,8,1152]{2,1,0:T(8,128)(2,1)S(1)}, u32[]{:S(2)}, u32[]{:S(2)}) async-start(bf16[8,8,1152]{2,1,0:T(8,128)(2,1)} %bitcast.2), calls=%async_computation | async-start | bytes 294912 | tf_op jit(solution)/shard_map/all_to_all | solution.py:108
  42.5 11.7 %all-to-all-start.1 = ((bf16[8,16,1152]{2,1,0:T(8,128)(2,1)}), bf16[8,16,1152]{2,1,0:T(8,128)(2,1)S(1)}, u32[]{:S(2)}, u32[]{:S(2)}) async-start(bf16[8,16,1152]{2,1,0:T(8,128)(2,1)} %bitcast.4), calls=%async_computation.1 | async-start | bytes 589824 | tf_op jit(solution)/shard_map/all_to_all | solution.py:108
  55.6 32.0 %copy-start.1 = (bf16[8,1152]{1,0:T(8,128)(2,1)S(1)}, bf16[8,1152]{1,0:T(8,128)(2,1)}, u32[]{:S(2)}) copy-start(bf16[8,1152]{1,0:T(8,128)(2,1)} %img_ref.3) | copy-start | bytes 55300
  66.4 21.2 %all-to-all-start.2 = ((bf16[8,8,1280]{2,1,0:T(8,128)(2,1)}), bf16[8,8,1280]{2,1,0:T(8,128)(2,1)S(1)}, u32[]{:S(2)}, u32[]{:S(2)}) async-start(bf16[8,8,1280]{2,1,0:T(8,128)(2,1)} %bitcast.6), calls=%async_computation.2 | async-start | bytes 327680 | tf_op jit(solution)/shard_map/all_to_all | solution.py:108
  71.0 16.7 %collective-permute-start.1 = (bf16[8,1152]{1,0:T(8,128)(2,1)S(1)}, bf16[8,1152]{1,0:T(8,128)(2,1)S(1)}, u32[]{:S(2)}, u32[]{:S(2)}) collective-permute-start(bf16[8,1152]{1,0:T(8,128)(2,1)S(1)} %get-tuple-element.14), channel_id=1, source_target_pairs={{0,960},{64,0},{128,64},{192,128},{256,192},{320,256},{384,320},{4... | collective-permute-start | bytes 55304 | tf_op jit(solution)/shard_map/ppermute | solution.py:23

commit v4 on v3

--- a/solution.py
+++ b/solution.py
@@ -38,7 +38,8 @@
     out_ref[...] = jnp.concatenate([img] * LINE).astype(out_ref.dtype)
 
 
-def pair_kernel(own_ref, before_ref, out_ref):
+def pair_kernel(own_ref, before_ref, after_ref, out_ref):
+    del after_ref
     pair = [own_ref[...].astype(jnp.float32), before_ref[...].astype(jnp.float32)]
     out_ref[...] = jnp.concatenate(pair * NEAR).astype(out_ref.dtype)
 
@@ -113,7 +114,6 @@
         out_shape=shape(LINE * ROWS, width, half),
         in_specs=[VMEM],
         out_specs=VMEM,
-        cost_estimate=pl.CostEstimate(flops=10**8, bytes_accessed=10**5, transcendentals=0),
         compiler_params=ROOM,
         name="spread",
     )(images)
@@ -121,13 +121,11 @@
     pairs = pl.pallas_call(
         pair_kernel,
         out_shape=shape(NEAR * 2 * ROWS, width, half),
-        in_specs=[VMEM, VMEM],
+        in_specs=[VMEM, VMEM, pl.BlockSpec(memory_space=pl.ANY)],
         out_specs=VMEM,
         compiler_params=ROOM,
-        cost_estimate=pl.CostEstimate(flops=2*10**10, bytes_accessed=10**6, transcendentals=0),
         name="pair",
-    )(texts, before)
-    pairs, line_imgs = lax.optimization_barrier((pairs, line_imgs))
+    )(texts, before, line_imgs)
     near_txts = exchange(pairs, ("core", "ring"), NEAR)
     gu_parts, gv_parts = pl.pallas_call(
         score_kernel,

time: 89.1 us -> 91.3 us (1.025)
  the two profiles are of different devices: /device:TPU:6 before, /device:TPU:134 now
where the time goes in v4:
time: 91.3 us; the launch traced here: 90.6 us
  starting transfers between devices  44.6 us (49%)
  waiting for transfers between devices  29 us (32%)
  blocking collectives  10.6 us (12%)
  Pallas kernels  3.75 us (4%)
  between operations  1.96 us (2%)
    all_to_all x3, starting transfers between devices, exchange(): return lax.all_to_all(pieces, axes, 0, 0, tiled=True).reshape(value.shape)  27 us
    ppermute x2, waiting for transfers between devices, next_chip(): lax.ppermute(value, CHIPS, [(s, (s + steps) % count) for s in range(count)])  23 us
    ppermute x2, starting transfers between devices, next_chip(): lax.ppermute(value, CHIPS, [(s, (s + steps) % count) for s in range(count)])  17.5 us
    all_to_all x1, blocking collectives, exchange(): return lax.all_to_all(pieces, axes, 0, 0, tiled=True).reshape(value.shape)  10.6 us
    all_to_all x3, waiting for transfers between devices, exchange(): return lax.all_to_all(pieces, axes, 0, 0, tiled=True).reshape(value.shape)  5.98 us
  transfers between devices with their start and end apart: 5, of which 3 were waited for; matrix products, arithmetic and copies ran while one was open for 0% of the time, Pallas kernels for 0%

profile of v4, /device:TPU:134, one launch (start us, length us, event | category | flops | bytes accessed | tf_op | source)
XLA Modules:
  0.0 90.6 jit_solution(538268336498874328)
XLA Ops:
  0.6 0.0 copy-start
  0.6 0.7 copy-done
  1.4 0.7 spread.1
  2.0 0.0 copy-start.2
  2.0 11.4 %all-to-all-start = ((bf16[8,8,1152]{2,1,0:T(8,128)(2,1)}), bf16[8,8,1152]{2,1,0:T(8,128)(2,1)S(1)}, u32[]{:S(2)}, u32[]{:S(2)}) async-start(bf16[8,8,1152]{2,1,0:T(8,128)(2,1)} %bitcast.2), calls=%async_computation | async-start | bytes 294912 | tf_op jit(solution)/shard_map/all_to_all | solution.py:109
  13.4 0.0 copy-done.2
  13.4 15.6 %collective-permute-start = (bf16[8,1152]{1,0:T(8,128)(2,1)S(1)}, bf16[8,1152]{1,0:T(8,128)(2,1)S(1)}, u32[]{:S(2)}, u32[]{:S(2)}) collective-permute-start(bf16[8,1152]{1,0:T(8,128)(2,1)S(1)} %copy-done.2), channel_id=1, source_target_pairs={{0,64},{64,128},{128,192},{192,256},{256,320},{320,384},{384,448},... | collective-permute-start | bytes 55304 | tf_op jit(solution)/shard_map/ppermute | solution.py:23
  29.1 1.4 %collective-permute-done.before_ref = bf16[8,1152]{1,0:T(8,128)(2,1)S(1)} collective-permute-done((bf16[8,1152]{1,0:T(8,128)(2,1)S(1)}, bf16[8,1152]{1,0:T(8,128)(2,1)S(1)}, u32[]{:S(2)}, u32[]{:S(2)}) %collective-permute-start) | collective-permute-done | bytes 18464 | tf_op jit(solution)/shard_map/ppermute | solution.py:23
  30.5 0.0 all-to-all-done
  30.5 0.7 pair.1
  31.3 5.2 %all-to-all-start.1 = ((bf16[8,16,1152]{2,1,0:T(8,128)(2,1)}), bf16[8,16,1152]{2,1,0:T(8,128)(2,1)S(1)}, u32[]{:S(2)}, u32[]{:S(2)}) async-start(bf16[8,16,1152]{2,1,0:T(8,128)(2,1)} %bitcast.4), calls=%async_computation.1 | async-start | bytes 589824 | tf_op jit(solution)/shard_map/all_to_all | solution.py:109
  37.8 6.0 %all-to-all-done.1 = bf16[8,16,1152]{2,1,0:T(8,128)(2,1)S(1)} async-done(((bf16[8,16,1152]{2,1,0:T(8,128)(2,1)}), bf16[8,16,1152]{2,1,0:T(8,128)(2,1)S(1)}, u32[]{:S(2)}, u32[]{:S(2)}) %all-to-all-start.1) | async-done | bytes 294944 | tf_op jit(solution)/shard_map/all_to_all | solution.py:109
  43.8 1.5 %score.1 = (bf16[64,1280]{1,0:T(8,128)(2,1)}, bf16[128,1152]{1,0:T(8,128)(2,1)S(1)}) custom-call(f32[1]{0:T(128)} %bitcast.10.scale_ref, f32[1]{0:T(128)} %bitcast.11.bias_ref, bf16[64,1152]{1,0:T(8,128)(2,1)S(1)} %bitcast.13, bf16[128,1152]{1,0:T(8,128)(2,1)S(1)} %bitcast.14), custom_call_target="tpu_custom_call" | custom-call | tf_op jit(solution)/shard_map/score/pallas_call | solution.py:130
  45.2 10.6 %all_to_all.20 = bf16[8,16,1152]{2,1,0:T(8,128)(2,1)S(1)} all-to-all(bf16[8,16,1152]{2,1,0:T(8,128)(2,1)S(1)} %bitcast.17), channel_id=1, replica_groups=mesh['far'=4,'x'=4,'core'=2,'line'=8,'ring'=4] {'core','ring'}, dimensions={0} | all-to-all | bytes 589824 | tf_op jit(solution)/shard_map/all_to_all | solution.py:109
  55.8 10.4 %all-to-all-start.2 = ((bf16[8,8,1280]{2,1,0:T(8,128)(2,1)}), bf16[8,8,1280]{2,1,0:T(8,128)(2,1)S(1)}, u32[]{:S(2)}, u32[]{:S(2)}) async-start(bf16[8,8,1280]{2,1,0:T(8,128)(2,1)} %bitcast.6), calls=%async_computation.2 | async-start | bytes 327680 | tf_op jit(solution)/shard_map/all_to_all | solution.py:109
  66.2 0.0 copy-start.1
  66.3 1.9 %collective-permute-start.1 = (bf16[8,1152]{1,0:T(8,128)(2,1)S(1)}, bf16[8,1152]{1,0:T(8,128)(2,1)S(1)}, u32[]{:S(2)}, u32[]{:S(2)}) collective-permute-start(bf16[8,1152]{1,0:T(8,128)(2,1)S(1)} %get-tuple-element.10), channel_id=1, source_target_pairs={{0,960},{64,0},{128,64},{192,128},{256,192},{320,256},{384,320},{4... | collective-permute-start | bytes 55304 | tf_op jit(solution)/shard_map/ppermute | solution.py:23
  68.2 21.6 %collective-permute-done.1.back_ref = bf16[8,1152]{1,0:T(8,128)(2,1)S(1)} collective-permute-done((bf16[8,1152]{1,0:T(8,128)(2,1)S(1)}, bf16[8,1152]{1,0:T(8,128)(2,1)S(1)}, u32[]{:S(2)}, u32[]{:S(2)}) %collective-permute-start.1) | collective-permute-done | bytes 18464 | tf_op jit(solution)/shard_map/ppermute | solution.py:23
  89.8 0.0 all-to-all-done.2
  89.8 0.0 copy-done.1
  89.8 0.8 finish.1
  (1 shorter events, 0.0 us)
Async XLA Ops:
  0.6 0.7 copy-start
  2.0 11.4 %copy-start.2 = (bf16[8,1152]{1,0:T(8,128)(2,1)S(1)}, bf16[8,1152]{1,0:T(8,128)(2,1)}, u32[]{:S(2)}) copy-start(bf16[8,1152]{1,0:T(8,128)(2,1)} %txt_ref.1) | copy-start | bytes 55300
  2.0 28.5 %all-to-all-start = ((bf16[8,8,1152]{2,1,0:T(8,128)(2,1)}), bf16[8,8,1152]{2,1,0:T(8,128)(2,1)S(1)}, u32[]{:S(2)}, u32[]{:S(2)}) async-start(bf16[8,8,1152]{2,1,0:T(8,128)(2,1)} %bitcast.2), calls=%async_computation | async-start | bytes 294912 | tf_op jit(solution)/shard_map/all_to_all | solution.py:109
  13.4 17.1 %collective-permute-start = (bf16[8,1152]{1,0:T(8,128)(2,1)S(1)}, bf16[8,1152]{1,0:T(8,128)(2,1)S(1)}, u32[]{:S(2)}, u32[]{:S(2)}) collective-permute-start(bf16[8,1152]{1,0:T(8,128)(2,1)S(1)} %copy-done.2), channel_id=1, source_target_pairs={{0,64},{64,128},{128,192},{192,256},{256,320},{320,384},{384,448},... | collective-permute-start | bytes 55304 | tf_op jit(solution)/shard_map/ppermute | solution.py:23
  31.3 12.5 %all-to-all-start.1 = ((bf16[8,16,1152]{2,1,0:T(8,128)(2,1)}), bf16[8,16,1152]{2,1,0:T(8,128)(2,1)S(1)}, u32[]{:S(2)}, u32[]{:S(2)}) async-start(bf16[8,16,1152]{2,1,0:T(8,128)(2,1)} %bitcast.4), calls=%async_computation.1 | async-start | bytes 589824 | tf_op jit(solution)/shard_map/all_to_all | solution.py:109
  55.8 34.0 %all-to-all-start.2 = ((bf16[8,8,1280]{2,1,0:T(8,128)(2,1)}), bf16[8,8,1280]{2,1,0:T(8,128)(2,1)S(1)}, u32[]{:S(2)}, u32[]{:S(2)}) async-start(bf16[8,8,1280]{2,1,0:T(8,128)(2,1)} %bitcast.6), calls=%async_computation.2 | async-start | bytes 327680 | tf_op jit(solution)/shard_map/all_to_all | solution.py:109
  66.2 23.6 %copy-start.1 = (bf16[8,1152]{1,0:T(8,128)(2,1)S(1)}, bf16[8,1152]{1,0:T(8,128)(2,1)}, u32[]{:S(2)}) copy-start(bf16[8,1152]{1,0:T(8,128)(2,1)} %img_ref.3) | copy-start | bytes 55300
  66.3 23.5 %collective-permute-start.1 = (bf16[8,1152]{1,0:T(8,128)(2,1)S(1)}, bf16[8,1152]{1,0:T(8,128)(2,1)S(1)}, u32[]{:S(2)}, u32[]{:S(2)}) collective-permute-start(bf16[8,1152]{1,0:T(8,128)(2,1)S(1)} %get-tuple-element.10), channel_id=1, source_target_pairs={{0,960},{64,0},{128,64},{192,128},{256,192},{320,256},{384,320},{4... | collective-permute-start | bytes 55304 | tf_op jit(solution)/shard_map/ppermute | solution.py:23

commit v5 on v4

--- a/solution.py
+++ b/solution.py
@@ -84,13 +84,16 @@
     back_ref[...] = total[ROWS:].astype(back_ref.dtype)
 
 
-def finish_kernel(parts_ref, img_ref, txt_ref, own_ref, back_ref, ig_ref, tg_ref, loss_ref):
+def finish_texts_kernel(txt_ref, own_ref, back_ref, tg_ref):
+    gv = own_ref[...] + back_ref[...].astype(jnp.float32)
+    tg_ref[...] = project_back(gv, *normalize(txt_ref[...]))
+
+
+def finish_images_kernel(parts_ref, img_ref, ig_ref, loss_ref):
     width = img_ref.shape[1]
     parts = parts_ref[...].astype(jnp.float32)
     total = jnp.sum(parts.reshape(LINE, ROWS, parts.shape[1]), axis=0)
     ig_ref[...] = project_back(total[:, :width], *normalize(img_ref[...]))
-    gv = own_ref[...] + back_ref[...].astype(jnp.float32)
-    tg_ref[...] = project_back(gv, *normalize(txt_ref[...]))
     loss = jnp.sum(total[:, width:], axis=1, keepdims=True)
     row = lax.broadcasted_iota(jnp.int32, (ROWS, ROWS), 0)
     lane = lax.broadcasted_iota(jnp.int32, (ROWS, ROWS), 1)
@@ -136,7 +139,6 @@
         name="score",
     )(scale.reshape(1), bias.reshape(1), line_imgs, near_txts)
     gv_parts = exchange(gv_parts, ("core", "ring"), NEAR)
-    gu_parts = exchange(gu_parts, "line", LINE)
     own, back = pl.pallas_call(
         near_sum_kernel,
         out_shape=(shape(ROWS, width, full), shape(ROWS, width, half)),
@@ -145,19 +147,27 @@
         compiler_params=ROOM,
         name="near_sum",
     )(gv_parts)
+    gu_parts, own, back = lax.optimization_barrier((gu_parts, own, back))
     back = next_chip(back, -1)
-    return pl.pallas_call(
-        finish_kernel,
-        out_shape=(
-            shape(ROWS, width, full),
-            shape(ROWS, width, full),
-            jax.ShapeDtypeStruct((ROWS,), full),
-        ),
-        in_specs=[VMEM] * 5,
-        out_specs=(VMEM, VMEM, VMEM),
+    gu_parts = exchange(gu_parts, "line", LINE)
+    text_grad = pl.pallas_call(
+        finish_texts_kernel,
+        out_shape=shape(ROWS, width, full),
+        in_specs=[VMEM] * 3,
+        out_specs=VMEM,
         compiler_params=ROOM,
-        name="finish",
-    )(gu_parts, images, texts, own, back)
+        cost_estimate=pl.CostEstimate(flops=2 * 10**10, bytes_accessed=10**6, transcendentals=0),
+        name="finish_texts",
+    )(texts, own, back)
+    image_grad, loss = pl.pallas_call(
+        finish_images_kernel,
+        out_shape=(shape(ROWS, width, full), jax.ShapeDtypeStruct((ROWS,), full)),
+        in_specs=[VMEM] * 2,
+        out_specs=(VMEM, VMEM),
+        compiler_params=ROOM,
+        name="finish_images",
+    )(gu_parts, images)
+    return image_grad, text_grad, loss
 
 
 def solution(mesh):

time: 91.3 us -> 89.1 us (0.976)
  the two profiles are of different devices: /device:TPU:134 before, /device:TPU:32 now
where the time goes in v5:
time: 89.1 us; the launch traced here: 88.5 us
  starting transfers between devices  37.2 us (42%)
  waiting for transfers between devices  33.5 us (38%)
  blocking collectives  10.6 us (12%)
  Pallas kernels  4.53 us (5%)
  between operations  1.97 us (2%)
    all_to_all x3, starting transfers between devices, exchange(): return lax.all_to_all(pieces, axes, 0, 0, tiled=True).reshape(value.shape)  27.2 us
    all_to_all x3, waiting for transfers between devices, exchange(): return lax.all_to_all(pieces, axes, 0, 0, tiled=True).reshape(value.shape)  17.5 us
    ppermute x2, waiting for transfers between devices, next_chip(): lax.ppermute(value, CHIPS, [(s, (s + steps) % count) for s in range(count)])  16 us
    all_to_all x1, blocking collectives, exchange(): return lax.all_to_all(pieces, axes, 0, 0, tiled=True).reshape(value.shape)  10.6 us
    ppermute x2, starting transfers between devices, next_chip(): lax.ppermute(value, CHIPS, [(s, (s + steps) % count) for s in range(count)])  9.97 us
  transfers between devices with their start and end apart: 5, of which 3 were waited for; matrix products, arithmetic and copies ran while one was open for 0% of the time, Pallas kernels for 1%

profile of v5, /device:TPU:32, one launch (start us, length us, event | category | flops | bytes accessed | tf_op | source)
XLA Modules:
  0.0 88.5 jit_solution(9260161520810023615)
XLA Ops:
  0.6 0.0 copy-start
  0.6 0.7 copy-done
  1.4 0.7 spread.1
  2.0 0.0 copy-start.2
  2.0 16.2 %all-to-all-start = ((bf16[8,8,1152]{2,1,0:T(8,128)(2,1)}), bf16[8,8,1152]{2,1,0:T(8,128)(2,1)S(1)}, u32[]{:S(2)}, u32[]{:S(2)}) async-start(bf16[8,8,1152]{2,1,0:T(8,128)(2,1)} %bitcast.2), calls=%async_computation | async-start | bytes 294912 | tf_op jit(solution)/shard_map/all_to_all | solution.py:112
  18.2 0.0 copy-done.2
  18.2 1.9 %collective-permute-start = (bf16[8,1152]{1,0:T(8,128)(2,1)S(1)}, bf16[8,1152]{1,0:T(8,128)(2,1)S(1)}, u32[]{:S(2)}, u32[]{:S(2)}) collective-permute-start(bf16[8,1152]{1,0:T(8,128)(2,1)S(1)} %copy-done.2), channel_id=1, source_target_pairs={{0,64},{64,128},{128,192},{192,256},{256,320},{320,384},{384,448},... | collective-permute-start | bytes 55304 | tf_op jit(solution)/shard_map/ppermute | solution.py:23
  20.1 16.0 %collective-permute-done.before_ref = bf16[8,1152]{1,0:T(8,128)(2,1)S(1)} collective-permute-done((bf16[8,1152]{1,0:T(8,128)(2,1)S(1)}, bf16[8,1152]{1,0:T(8,128)(2,1)S(1)}, u32[]{:S(2)}, u32[]{:S(2)}) %collective-permute-start) | collective-permute-done | bytes 18464 | tf_op jit(solution)/shard_map/ppermute | solution.py:23
  36.2 0.0 all-to-all-done
  36.2 0.7 pair.1
  36.9 4.5 %all-to-all-start.1 = ((bf16[8,16,1152]{2,1,0:T(8,128)(2,1)}), bf16[8,16,1152]{2,1,0:T(8,128)(2,1)S(1)}, u32[]{:S(2)}, u32[]{:S(2)}) async-start(bf16[8,16,1152]{2,1,0:T(8,128)(2,1)} %bitcast.4), calls=%async_computation.1 | async-start | bytes 589824 | tf_op jit(solution)/shard_map/all_to_all | solution.py:112
  42.7 6.0 %all-to-all-done.1 = bf16[8,16,1152]{2,1,0:T(8,128)(2,1)S(1)} async-done(((bf16[8,16,1152]{2,1,0:T(8,128)(2,1)}), bf16[8,16,1152]{2,1,0:T(8,128)(2,1)S(1)}, u32[]{:S(2)}, u32[]{:S(2)}) %all-to-all-start.1) | async-done | bytes 294944 | tf_op jit(solution)/shard_map/all_to_all | solution.py:112
  48.6 1.5 %score.1 = (bf16[64,1280]{1,0:T(8,128)(2,1)}, bf16[128,1152]{1,0:T(8,128)(2,1)S(1)}) custom-call(f32[1]{0:T(128)} %bitcast.10.scale_ref, f32[1]{0:T(128)} %bitcast.11.bias_ref, bf16[64,1152]{1,0:T(8,128)(2,1)S(1)} %bitcast.13, bf16[128,1152]{1,0:T(8,128)(2,1)S(1)} %bitcast.14), custom_call_target="tpu_custom_call" | custom-call | tf_op jit(solution)/shard_map/score/pallas_call | solution.py:133
  50.1 10.6 %all_to_all.20 = bf16[8,16,1152]{2,1,0:T(8,128)(2,1)S(1)} all-to-all(bf16[8,16,1152]{2,1,0:T(8,128)(2,1)S(1)} %bitcast.17), channel_id=1, replica_groups=mesh['far'=4,'x'=4,'core'=2,'line'=8,'ring'=4] {'core','ring'}, dimensions={0} | all-to-all | bytes 589824 | tf_op jit(solution)/shard_map/all_to_all | solution.py:112
  60.8 8.1 %collective-permute-start.1 = (bf16[8,1152]{1,0:T(8,128)(2,1)S(1)}, bf16[8,1152]{1,0:T(8,128)(2,1)S(1)}, u32[]{:S(2)}, u32[]{:S(2)}) collective-permute-start(bf16[8,1152]{1,0:T(8,128)(2,1)S(1)} %get-tuple-element.19), channel_id=1, source_target_pairs={{0,960},{64,0},{128,64},{192,128},{256,192},{320,256},{384,320},{4... | collective-permute-start | bytes 55304 | tf_op jit(solution)/shard_map/ppermute | solution.py:23
  68.8 6.6 %all-to-all-start.3 = ((bf16[8,8,1280]{2,1,0:T(8,128)(2,1)}), bf16[8,8,1280]{2,1,0:T(8,128)(2,1)S(1)}, u32[]{:S(2)}, u32[]{:S(2)}) async-start(bf16[8,8,1280]{2,1,0:T(8,128)(2,1)} %bitcast.8), calls=%async_computation.3 | async-start | bytes 327680 | tf_op jit(solution)/shard_map/all_to_all | solution.py:112
  75.4 0.0 copy-start.1
  75.4 0.0 collective-permute-done.1.back_ref
  75.4 0.8 finish_texts.1
  76.2 11.5 %all-to-all-done.3 = bf16[8,8,1280]{2,1,0:T(8,128)(2,1)S(1)} async-done(((bf16[8,8,1280]{2,1,0:T(8,128)(2,1)}), bf16[8,8,1280]{2,1,0:T(8,128)(2,1)S(1)}, u32[]{:S(2)}, u32[]{:S(2)}) %all-to-all-start.3) | async-done | bytes 163872 | tf_op jit(solution)/shard_map/all_to_all | solution.py:112
  87.7 0.0 copy-done.1
  87.7 0.8 finish_images.1
  (1 shorter events, 0.0 us)
Async XLA Ops:
  0.6 0.7 copy-start
  2.0 16.2 %copy-start.2 = (bf16[8,1152]{1,0:T(8,128)(2,1)S(1)}, bf16[8,1152]{1,0:T(8,128)(2,1)}, u32[]{:S(2)}) copy-start(bf16[8,1152]{1,0:T(8,128)(2,1)} %txt_ref.1) | copy-start | bytes 55300
  2.0 34.1 %all-to-all-start = ((bf16[8,8,1152]{2,1,0:T(8,128)(2,1)}), bf16[8,8,1152]{2,1,0:T(8,128)(2,1)S(1)}, u32[]{:S(2)}, u32[]{:S(2)}) async-start(bf16[8,8,1152]{2,1,0:T(8,128)(2,1)} %bitcast.2), calls=%async_computation | async-start | bytes 294912 | tf_op jit(solution)/shard_map/all_to_all | solution.py:112
  18.2 18.0 %collective-permute-start = (bf16[8,1152]{1,0:T(8,128)(2,1)S(1)}, bf16[8,1152]{1,0:T(8,128)(2,1)S(1)}, u32[]{:S(2)}, u32[]{:S(2)}) collective-permute-start(bf16[8,1152]{1,0:T(8,128)(2,1)S(1)} %copy-done.2), channel_id=1, source_target_pairs={{0,64},{64,128},{128,192},{192,256},{256,320},{320,384},{384,448},... | collective-permute-start | bytes 55304 | tf_op jit(solution)/shard_map/ppermute | solution.py:23
  36.9 11.7 %all-to-all-start.1 = ((bf16[8,16,1152]{2,1,0:T(8,128)(2,1)}), bf16[8,16,1152]{2,1,0:T(8,128)(2,1)S(1)}, u32[]{:S(2)}, u32[]{:S(2)}) async-start(bf16[8,16,1152]{2,1,0:T(8,128)(2,1)} %bitcast.4), calls=%async_computation.1 | async-start | bytes 589824 | tf_op jit(solution)/shard_map/all_to_all | solution.py:112
  60.8 14.7 %collective-permute-start.1 = (bf16[8,1152]{1,0:T(8,128)(2,1)S(1)}, bf16[8,1152]{1,0:T(8,128)(2,1)S(1)}, u32[]{:S(2)}, u32[]{:S(2)}) collective-permute-start(bf16[8,1152]{1,0:T(8,128)(2,1)S(1)} %get-tuple-element.19), channel_id=1, source_target_pairs={{0,960},{64,0},{128,64},{192,128},{256,192},{320,256},{384,320},{4... | collective-permute-start | bytes 55304 | tf_op jit(solution)/shard_map/ppermute | solution.py:23
  68.8 18.9 %all-to-all-start.3 = ((bf16[8,8,1280]{2,1,0:T(8,128)(2,1)}), bf16[8,8,1280]{2,1,0:T(8,128)(2,1)S(1)}, u32[]{:S(2)}, u32[]{:S(2)}) async-start(bf16[8,8,1280]{2,1,0:T(8,128)(2,1)} %bitcast.8), calls=%async_computation.3 | async-start | bytes 327680 | tf_op jit(solution)/shard_map/all_to_all | solution.py:112
  75.4 12.3 %copy-start.1 = (bf16[8,1152]{1,0:T(8,128)(2,1)S(1)}, bf16[8,1152]{1,0:T(8,128)(2,1)}, u32[]{:S(2)}) copy-start(bf16[8,1152]{1,0:T(8,128)(2,1)} %img_ref.3) | copy-start | bytes 55300

commit v6 on v4

v6 whole, which is shorter than its diff:
```python
import jax
import jax.numpy as jnp
from jax import lax
from jax.experimental import pallas as pl
from jax.experimental.pallas import tpu as pltpu
from jax.sharding import Mesh, PartitionSpec as P

EPS = 1e-06
ROUNDS = 3
ROWS = 8
AXES = ("far", "x", "core", "line", "ring")
FAR, X, CORE, LINE, RING = 4, 4, 2, 8, 4
CHIPS = ("far", "x")
SHARE = ROUNDS * ROWS
LANES = 128
SMEM = pl.BlockSpec(memory_space=pltpu.SMEM)
VMEM = pl.BlockSpec(memory_space=pltpu.VMEM)
ROOM = pltpu.CompilerParams(vmem_limit_bytes=8 * 2**20)


def next_chip(value, steps):
    count = FAR * X
    return lax.ppermute(value, CHIPS, [(s, (s + steps) % count) for s in range(count)])


def normalize(x):
    xf = x.astype(jnp.float32)
    norms = jnp.sqrt(jnp.sum(xf * xf, axis=-1, keepdims=True) + EPS)
    return xf / norms, norms


def project_back(grad, unit, norms):
    return (grad - unit * jnp.sum(unit * grad, axis=-1, keepdims=True)) / norms


def spread_kernel(img_ref, txt_ref, out_ref):
    width = img_ref.shape[1]
    for ref, columns in ((img_ref, slice(0, width)), (txt_ref, slice(width, 2 * width))):
        shard = ref[...].astype(jnp.float32)
        out_ref[:, columns] = jnp.concatenate([shard] * LINE).astype(out_ref.dtype)


def mate_kernel(img_ref, txt_ref, after_ref, before_ref, out_ref):
    first = lax.axis_index("core") == 0
    img, txt, after, before = (
        ref[...].astype(jnp.float32) for ref in (img_ref, txt_ref, after_ref, before_ref)
    )
    pair = [jnp.where(first, txt, before), jnp.where(first, after, img)]
    out_ref[...] = jnp.concatenate(pair).astype(out_ref.dtype)


def pack_kernel(img_ref, txt_ref, after_ref, before_ref, mate_ref, out_ref):
    img, txt, after, before, mate = (
        ref[...].astype(jnp.float32) for ref in (img_ref, txt_ref, after_ref, before_ref, mate_ref)
    )
    parts = [txt, mate[:ROWS], before, img, mate[ROWS:], after]
    out_ref[...] = jnp.concatenate(parts).astype(out_ref.dtype)


def score_kernel(scale_ref, bias_ref, line_ref, ring_ref, out_ref):
    scale, bias = scale_ref[0], bias_ref[0]
    line, ring = lax.axis_index("line"), lax.axis_index("ring")
    width = ring_ref.shape[1]
    around = normalize(ring_ref[...])[0].reshape(RING, 2, SHARE, width)

    def against(ours, others):
        ours = normalize(ours)[0].astype(jnp.bfloat16)
        others = others.reshape(RING * SHARE, width).astype(jnp.bfloat16)
        dots = lax.dot_general(
            ours, others, (((1,), (1,)), ((), ())), preferred_element_type=jnp.float32
        )
        logit = scale * dots + bias
        row = lax.broadcasted_iota(jnp.int32, logit.shape, 0) - line * ROWS
        column = lax.broadcasted_iota(jnp.int32, logit.shape, 1) - ring * SHARE
        own = (row == column) & (row >= 0) & (row < ROWS)
        signed = jnp.where(own, -logit, logit)
        decay = jnp.exp(-jnp.abs(signed))
        chance = jnp.where(signed >= 0, 1.0, decay) / (1.0 + decay)
        coef = jnp.where(own, -chance, chance) * scale
        grad = jnp.dot(coef.astype(jnp.bfloat16), others, preferred_element_type=jnp.float32)
        return grad.astype(jnp.bfloat16), signed, decay

    out_ref[:, width : 2 * width] = against(line_ref[:, width:], around[:, 1])[0]
    grad, signed, decay = against(line_ref[:, :width], around[:, 0])
    out_ref[:, :width] = grad
    loss = jnp.maximum(signed, 0.0) + jnp.log1p(decay)
    total = jnp.sum(loss, axis=1, keepdims=True)
    high = total.astype(jnp.bfloat16).astype(jnp.float32)
    lane = lax.broadcasted_iota(jnp.int32, (total.shape[0], LANES), 1)
    out_ref[:, 2 * width :] = jnp.where(
        lane == 0, high, jnp.where(lane == 1, total - high, 0.0)
    ).astype(jnp.bfloat16)


def finish_kernel(parts_ref, img_ref, txt_ref, ig_ref, tg_ref, loss_ref):
    width = img_ref.shape[1]
    parts = parts_ref[...].astype(jnp.float32)
    total = jnp.sum(parts.reshape(LINE, ROWS, parts.shape[1]), axis=0)
    ig_ref[...] = project_back(total[:, :width], *normalize(img_ref[...]))
    tg_ref[...] = project_back(total[:, width : 2 * width], *normalize(txt_ref[...]))
    loss = jnp.sum(total[:, 2 * width :], axis=1, keepdims=True)
    row = lax.broadcasted_iota(jnp.int32, (ROWS, ROWS), 0)
    lane = lax.broadcasted_iota(jnp.int32, (ROWS, ROWS), 1)
    loss_ref[...] = jnp.sum(jnp.where(row == lane, loss, 0.0), axis=0)


def on_device(images, texts, scale, bias):
    width = images.shape[1]
    half, full = jnp.bfloat16, jnp.float32

    def shape(rows, columns, kind):
        return jax.ShapeDtypeStruct((rows, columns), kind)

    def line_exchange(value):
        pieces = value.reshape(LINE, ROWS, value.shape[1])
        return lax.all_to_all(pieces, "line", 0, 0, tiled=True).reshape(value.shape)

    before = next_chip(texts, 1)
    after = next_chip(images, -1)
    spread = pl.pallas_call(
        spread_kernel,
        out_shape=shape(LINE * ROWS, 2 * width, half),
        in_specs=[VMEM] * 2,
        out_specs=VMEM,
        compiler_params=ROOM,
        name="spread",
    )(images, texts)
    line = line_exchange(spread)
    mate = pl.pallas_call(
        mate_kernel,
        out_shape=shape(2 * ROWS, width, half),
        in_specs=[VMEM] * 4,
        out_specs=VMEM,
        compiler_params=ROOM,
        cost_estimate=pl.CostEstimate(flops=2 * 10**10, bytes_accessed=10**6, transcendentals=0),
        name="mate",
    )(images, texts, after, before)
    mate = lax.ppermute(mate, "core", [(0, 1), (1, 0)])
    pack = pl.pallas_call(
        pack_kernel,
        out_shape=shape(2 * SHARE, width, half),
        in_specs=[VMEM] * 5,
        out_specs=VMEM,
        compiler_params=ROOM,
        name="pack",
    )(images, texts, after, before, mate)
    ring = lax.all_gather(pack, "ring", axis=0, tiled=True)
    parts = pl.pallas_call(
        score_kernel,
        out_shape=shape(LINE * ROWS, 2 * width + LANES, half),
        in_specs=[SMEM, SMEM, VMEM, VMEM],
        out_specs=VMEM,
        compiler_params=ROOM,
        name="score",
    )(scale.reshape(1), bias.reshape(1), line, ring)
    parts = line_exchange(parts)
    return pl.pallas_call(
        finish_kernel,
        out_shape=(
            shape(ROWS, width, full),
            shape(ROWS, width, full),
            jax.ShapeDtypeStruct((ROWS,), full),
        ),
        in_specs=[VMEM] * 3,
        out_specs=(VMEM, VMEM, VMEM),
        compiler_params=ROOM,
        name="finish",
    )(parts, images, texts)


def solution(mesh):
    parts = Mesh(mesh.devices.reshape(FAR, X, CORE, LINE, RING), AXES)
    rows = P(AXES, None)
    return jax.shard_map(
        on_device,
        mesh=parts,
        in_specs=(rows, rows, P(), P()),
        out_specs=(rows, rows, P(AXES)),
        check_vma=False,
    )
```

time: 91.3 us -> 83.8 us (0.918)
  the two profiles are of different devices: /device:TPU:134 before, /device:TPU:8 now
where the time goes in v6:
time: 83.8 us; the launch traced here: 83.2 us
  blocking collectives  35.8 us (43%)
  starting transfers between devices  34.2 us (41%)
  waiting for transfers between devices  7.41 us (9%)
  Pallas kernels  2.4 us (3%)
  between operations  2 us (2%)
  local copies, waits for them, and re-layouts  1.45 us (2%)
    ppermute x2, starting transfers between devices, next_chip(): lax.ppermute(value, CHIPS, [(s, (s + steps) % count) for s in range(count)])  27.1 us
    all_to_all x1, blocking collectives, line_exchange(): return lax.all_to_all(pieces, 'line', 0, 0, tiled=True).reshape(value.shape)  22.8 us
    all_gather x1, blocking collectives, on_device(): ring = lax.all_gather(pack, 'ring', axis=0, tiled=True)  13 us
    ppermute x2, waiting for transfers between devices, next_chip(): lax.ppermute(value, CHIPS, [(s, (s + steps) % count) for s in range(count)])  7.41 us
    all_to_all x1, starting transfers between devices, line_exchange(): return lax.all_to_all(pieces, 'line', 0, 0, tiled=True).reshape(value.shape)  5.15 us
    ppermute x1, starting transfers between devices, on_device(): mate = lax.ppermute(mate, 'core', [(0, 1), (1, 0)])  1.92 us
  transfers between devices with their start and end apart: 4, of which 1 were waited for; matrix products, arithmetic and copies ran while one was open for 0% of the time, Pallas kernels for 1%

profile of v6, /device:TPU:8, one launch (start us, length us, event | category | flops | bytes accessed | tf_op | source)
XLA Modules:
  0.0 83.2 jit_solution(678809352717960320)
XLA Ops:
  0.6 25.2 %collective-permute-start = (bf16[8,1152]{1,0:T(8,128)(2,1)}, bf16[8,1152]{1,0:T(8,128)(2,1)S(1)}, u32[]{:S(2)}, u32[]{:S(2)}) collective-permute-start(bf16[8,1152]{1,0:T(8,128)(2,1)} %img_ref.7), channel_id=1, source_target_pairs={{0,960},{64,0},{128,64},{192,128},{256,192},{320,256},{384,320},{4... | collective-permute-start | bytes 55304 | tf_op jit(solution)/shard_map/ppermute | solution.py:23
  25.8 1.9 %collective-permute-start.1 = (bf16[8,1152]{1,0:T(8,128)(2,1)}, bf16[8,1152]{1,0:T(8,128)(2,1)S(1)}, u32[]{:S(2)}, u32[]{:S(2)}) collective-permute-start(bf16[8,1152]{1,0:T(8,128)(2,1)} %txt_ref.7), channel_id=1, source_target_pairs={{0,64},{64,128},{128,192},{192,256},{256,320},{320,384},{384,448},... | collective-permute-start | bytes 55304 | tf_op jit(solution)/shard_map/ppermute | solution.py:23
  27.8 0.0 copy-start
  27.8 0.7 copy-done
  28.5 0.0 copy-start.2
  28.5 0.7 copy-done.2
  29.2 0.7 spread.1
  30.0 0.0 copy-start.1
  30.0 0.0 copy-start.3
  30.0 5.2 %all-to-all-start = ((bf16[8,8,2304]{2,1,0:T(8,128)(2,1)}), bf16[8,8,2304]{2,1,0:T(8,128)(2,1)S(1)}, u32[]{:S(2)}, u32[]{:S(2)}) async-start(bf16[8,8,2304]{2,1,0:T(8,128)(2,1)} %bitcast.2), calls=%async_computation | async-start | bytes 589824 | tf_op jit(solution)/shard_map/all_to_all | solution.py:116
  35.1 0.0 collective-permute-done.after_ref
  35.1 7.4 %collective-permute-done.1.before_ref = bf16[8,1152]{1,0:T(8,128)(2,1)S(1)} collective-permute-done((bf16[8,1152]{1,0:T(8,128)(2,1)}, bf16[8,1152]{1,0:T(8,128)(2,1)S(1)}, u32[]{:S(2)}, u32[]{:S(2)}) %collective-permute-start.1) | collective-permute-done | bytes 18464 | tf_op jit(solution)/shard_map/ppermute | solution.py:23
  42.5 0.0 copy-done.1
  42.5 0.0 copy-done.3
  42.5 1.9 %collective-permute-start.2 = (bf16[16,1152]{1,0:T(8,128)(2,1)S(1)}, bf16[16,1152]{1,0:T(8,128)(2,1)S(1)}, u32[]{:S(2)}, u32[]{:S(2)}) collective-permute-start(bf16[16,1152]{1,0:T(8,128)(2,1)S(1)} %mate.1), channel_id=1, source_target_pairs={{0,32},{32,0},{1,33},{33,1},{2,34},{34,2},{3,35},{35,3},{4,36},{36... | collective-permute-start | bytes 110600 | tf_op jit(solution)/shard_map/ppermute | solution.py:138
  45.8 0.0 collective-permute-done.2.mate_ref
  45.8 13.0 %all_gather.3.ring_ref = bf16[192,1152]{1,0:T(8,128)(2,1)S(1)} all-gather(bf16[48,1152]{1,0:T(8,128)(2,1)S(1)} %pack.1), channel_id=1, replica_groups=mesh['far'=4,'x'=4,'core'=2,'line'=8,'ring'=4] {'ring'}, dimensions={0}, use_global_device_ids=true | all-gather | bytes 552960 | tf_op jit(solution)/shard_map/all_gather | solution.py:147
  58.8 0.0 all-to-all-done
  58.8 0.8 score.1
  59.6 22.8 %all_to_all.10 = bf16[8,8,2432]{2,1,0:T(8,128)(2,1)S(1)} all-to-all(bf16[8,8,2432]{2,1,0:T(8,128)(2,1)S(1)} %bitcast.8), channel_id=1, replica_groups=mesh['far'=4,'x'=4,'core'=2,'line'=8,'ring'=4] {'line'}, dimensions={0} | all-to-all | bytes 622592 | tf_op jit(solution)/shard_map/all_to_all | solution.py:116
  82.4 0.8 finish.1
  (2 shorter events, 0.0 us)
Async XLA Ops:
  0.6 34.5 %collective-permute-start = (bf16[8,1152]{1,0:T(8,128)(2,1)}, bf16[8,1152]{1,0:T(8,128)(2,1)S(1)}, u32[]{:S(2)}, u32[]{:S(2)}) collective-permute-start(bf16[8,1152]{1,0:T(8,128)(2,1)} %img_ref.7), channel_id=1, source_target_pairs={{0,960},{64,0},{128,64},{192,128},{256,192},{320,256},{384,320},{4... | collective-permute-start | bytes 55304 | tf_op jit(solution)/shard_map/ppermute | solution.py:23
  25.8 16.7 %collective-permute-start.1 = (bf16[8,1152]{1,0:T(8,128)(2,1)}, bf16[8,1152]{1,0:T(8,128)(2,1)S(1)}, u32[]{:S(2)}, u32[]{:S(2)}) collective-permute-start(bf16[8,1152]{1,0:T(8,128)(2,1)} %txt_ref.7), channel_id=1, source_target_pairs={{0,64},{64,128},{128,192},{192,256},{256,320},{320,384},{384,448},... | collective-permute-start | bytes 55304 | tf_op jit(solution)/shard_map/ppermute | solution.py:23
  27.8 0.7 copy-start
  28.5 0.7 copy-start.2
  30.0 12.6 %copy-start.1 = (bf16[8,1152]{1,0:T(8,128)(2,1)S(1)}, bf16[8,1152]{1,0:T(8,128)(2,1)}, u32[]{:S(2)}) copy-start(bf16[8,1152]{1,0:T(8,128)(2,1)} %img_ref.7) | copy-start | bytes 55300
  30.0 12.6 %copy-start.3 = (bf16[8,1152]{1,0:T(8,128)(2,1)S(1)}, bf16[8,1152]{1,0:T(8,128)(2,1)}, u32[]{:S(2)}) copy-start(bf16[8,1152]{1,0:T(8,128)(2,1)} %txt_ref.7) | copy-start | bytes 55300
  30.0 28.8 %all-to-all-start = ((bf16[8,8,2304]{2,1,0:T(8,128)(2,1)}), bf16[8,8,2304]{2,1,0:T(8,128)(2,1)S(1)}, u32[]{:S(2)}, u32[]{:S(2)}) async-start(bf16[8,8,2304]{2,1,0:T(8,128)(2,1)} %bitcast.2), calls=%async_computation | async-start | bytes 589824 | tf_op jit(solution)/shard_map/all_to_all | solution.py:116
  42.5 3.2 %collective-permute-start.2 = (bf16[16,1152]{1,0:T(8,128)(2,1)S(1)}, bf16[16,1152]{1,0:T(8,128)(2,1)S(1)}, u32[]{:S(2)}, u32[]{:S(2)}) collective-permute-start(bf16[16,1152]{1,0:T(8,128)(2,1)S(1)} %mate.1), channel_id=1, source_target_pairs={{0,32},{32,0},{1,33},{33,1},{2,34},{34,2},{3,35},{35,3},{4,36},{36... | collective-permute-start | bytes 110600 | tf_op jit(solution)/shard_map/ppermute | solution.py:138

commit v7 on v6

--- a/solution.py
+++ b/solution.py
@@ -18,9 +18,10 @@
 ROOM = pltpu.CompilerParams(vmem_limit_bytes=8 * 2**20)
 
 
-def next_chip(value, steps):
+def with_neighbour(value, first):
     count = FAR * X
-    return lax.ppermute(value, CHIPS, [(s, (s + steps) % count) for s in range(count)])
+    pairs = [(chip, (chip + 1) % count) for chip in range(first, count, 2)]
+    return lax.ppermute(value, CHIPS, pairs + [(b, a) for a, b in pairs])
 
 
 def normalize(x):
@@ -40,19 +41,23 @@
         out_ref[:, columns] = jnp.concatenate([shard] * LINE).astype(out_ref.dtype)
 
 
-def mate_kernel(img_ref, txt_ref, after_ref, before_ref, out_ref):
+def visitors(near, far):
+    even = (lax.axis_index("x") & 1) == 0
+    near, far = near.astype(jnp.float32), far.astype(jnp.float32)
+    return jnp.where(even, near, far), jnp.where(even, far, near)
+
+
+def mate_kernel(img_ref, txt_ref, near_ref, far_ref, out_ref):
     first = lax.axis_index("core") == 0
-    img, txt, after, before = (
-        ref[...].astype(jnp.float32) for ref in (img_ref, txt_ref, after_ref, before_ref)
-    )
+    img, txt = img_ref[...].astype(jnp.float32), txt_ref[...].astype(jnp.float32)
+    after, before = visitors(near_ref[...], far_ref[...])
     pair = [jnp.where(first, txt, before), jnp.where(first, after, img)]
     out_ref[...] = jnp.concatenate(pair).astype(out_ref.dtype)
 
 
-def pack_kernel(img_ref, txt_ref, after_ref, before_ref, mate_ref, out_ref):
-    img, txt, after, before, mate = (
-        ref[...].astype(jnp.float32) for ref in (img_ref, txt_ref, after_ref, before_ref, mate_ref)
-    )
+def pack_kernel(img_ref, txt_ref, near_ref, far_ref, mate_ref, out_ref):
+    img, txt, mate = (ref[...].astype(jnp.float32) for ref in (img_ref, txt_ref, mate_ref))
+    after, before = visitors(near_ref[...], far_ref[...])
     parts = [txt, mate[:ROWS], before, img, mate[ROWS:], after]
     out_ref[...] = jnp.concatenate(parts).astype(out_ref.dtype)
 
@@ -115,14 +120,14 @@
         pieces = value.reshape(LINE, ROWS, value.shape[1])
         return lax.all_to_all(pieces, "line", 0, 0, tiled=True).reshape(value.shape)
 
-    before = next_chip(texts, 1)
-    after = next_chip(images, -1)
+    even = (lax.axis_index("x") & 1) == 0
+    far = with_neighbour(jnp.where(even, images, texts), 1)
+    near = with_neighbour(jnp.where(even, texts, images), 0)
     spread = pl.pallas_call(
         spread_kernel,
         out_shape=shape(LINE * ROWS, 2 * width, half),
         in_specs=[VMEM] * 2,
         out_specs=VMEM,
-        compiler_params=ROOM,
         name="spread",
     )(images, texts)
     line = line_exchange(spread)
@@ -134,7 +139,7 @@
         compiler_params=ROOM,
         cost_estimate=pl.CostEstimate(flops=2 * 10**10, bytes_accessed=10**6, transcendentals=0),
         name="mate",
-    )(images, texts, after, before)
+    )(images, texts, near, far)
     mate = lax.ppermute(mate, "core", [(0, 1), (1, 0)])
     pack = pl.pallas_call(
         pack_kernel,
@@ -143,7 +148,7 @@
         out_specs=VMEM,
         compiler_params=ROOM,
         name="pack",
-    )(images, texts, after, before, mate)
+    )(images, texts, near, far, mate)
     ring = lax.all_gather(pack, "ring", axis=0, tiled=True)
     parts = pl.pallas_call(
         score_kernel,

time: 83.8 us -> 81.9 us (0.977)
  the two profiles are of different devices: /device:TPU:8 before, /device:TPU:2 now
where the time goes in v7:
time: 81.9 us; the launch traced here: 81.4 us
  blocking collectives  40.1 us (49%)
  starting transfers between devices  34.7 us (42%)
  Pallas kernels  3.15 us (4%)
  between operations  2.02 us (2%)
    ppermute x2, starting transfers between devices, with_neighbour(): return lax.ppermute(value, CHIPS, pairs + [(b, a) for a, b in pairs])  27.6 us
    all_to_all x1, blocking collectives, line_exchange(): return lax.all_to_all(pieces, 'line', 0, 0, tiled=True).reshape(value.shape)  26.8 us
    all_gather x1, blocking collectives, on_device(): ring = lax.all_gather(pack, 'ring', axis=0, tiled=True)  13.3 us
    all_to_all x1, starting transfers between devices, line_exchange(): return lax.all_to_all(pieces, 'line', 0, 0, tiled=True).reshape(value.shape)  5.15 us
    ppermute x1, starting transfers between devices, on_device(): mate = lax.ppermute(mate, 'core', [(0, 1), (1, 0)])  1.92 us
  transfers between devices with their start and end apart: 4, of which 1 were waited for; matrix products, arithmetic and copies ran while one was open for 0% of the time, Pallas kernels for 2%

profile of v7, /device:TPU:2, one launch (start us, length us, event | category | flops | bytes accessed | tf_op | source)
XLA Modules:
  0.0 81.4 jit_solution(8338219150474524679)
XLA Ops:
  0.6 0.7 broadcast_select_fusion
  1.4 3.4 %collective-permute-start.1 = (bf16[8,1152]{1,0:T(8,128)(2,1)S(1)}, bf16[8,1152]{1,0:T(8,128)(2,1)S(1)}, u32[]{:S(2)}, u32[]{:S(2)}) collective-permute-start(bf16[8,1152]{1,0:T(8,128)(2,1)S(1)} %get-tuple-element.3), channel_id=1, source_target_pairs={{64,128},{192,256},{320,384},{448,512},{576,640},{704,768},{832,89... | collective-permute-start | bytes 55304 | tf_op jit(solution)/shard_map/ppermute | solution.py:24
  4.8 24.2 %collective-permute-start = (bf16[8,1152]{1,0:T(8,128)(2,1)S(1)}, bf16[8,1152]{1,0:T(8,128)(2,1)S(1)}, u32[]{:S(2)}, u32[]{:S(2)}) collective-permute-start(bf16[8,1152]{1,0:T(8,128)(2,1)S(1)} %get-tuple-element.4), channel_id=1, source_target_pairs={{0,64},{128,192},{256,320},{384,448},{512,576},{640,704},{768,832}... | collective-permute-start | bytes 55304 | tf_op jit(solution)/shard_map/ppermute | solution.py:24
  29.0 1.5 %spread.1 = bf16[64,2304]{1,0:T(8,128)(2,1)} custom-call(bf16[8,1152]{1,0:T(8,128)(2,1)} %img_ref.7, bf16[8,1152]{1,0:T(8,128)(2,1)} %txt_ref.7), custom_call_target="tpu_custom_call" | custom-call | tf_op jit(solution)/shard_map/spread/pallas_call | solution.py:126
  30.5 0.0 copy-start
  30.5 0.0 copy-start.1
  30.5 5.2 %all-to-all-start = ((bf16[8,8,2304]{2,1,0:T(8,128)(2,1)}), bf16[8,8,2304]{2,1,0:T(8,128)(2,1)S(1)}, u32[]{:S(2)}, u32[]{:S(2)}) async-start(bf16[8,8,2304]{2,1,0:T(8,128)(2,1)} %bitcast.11), calls=%async_computation | async-start | bytes 589824 | tf_op jit(solution)/shard_map/all_to_all | solution.py:121
  35.7 0.0 collective-permute-done.1.far_ref
  35.7 0.0 collective-permute-done.near_ref
  35.7 0.0 copy-done
  35.7 0.0 copy-done.1
  35.7 1.9 %collective-permute-start.2 = (bf16[16,1152]{1,0:T(8,128)(2,1)S(1)}, bf16[16,1152]{1,0:T(8,128)(2,1)S(1)}, u32[]{:S(2)}, u32[]{:S(2)}) collective-permute-start(bf16[16,1152]{1,0:T(8,128)(2,1)S(1)} %mate.1), channel_id=1, source_target_pairs={{0,32},{32,0},{1,33},{33,1},{2,34},{34,2},{3,35},{35,3},{4,36},{36... | collective-permute-start | bytes 110600 | tf_op jit(solution)/shard_map/ppermute | solution.py:143
  38.9 0.0 collective-permute-done.2.mate_ref
  39.0 13.3 %all_gather.3.ring_ref = bf16[192,1152]{1,0:T(8,128)(2,1)S(1)} all-gather(bf16[48,1152]{1,0:T(8,128)(2,1)S(1)} %pack.1), channel_id=1, replica_groups=mesh['far'=4,'x'=4,'core'=2,'line'=8,'ring'=4] {'ring'}, dimensions={0}, use_global_device_ids=true | all-gather | bytes 552960 | tf_op jit(solution)/shard_map/all_gather | solution.py:152
  52.2 0.7 all-to-all-done
  53.0 0.8 score.1
  53.8 26.8 %all_to_all.10 = bf16[8,8,2432]{2,1,0:T(8,128)(2,1)S(1)} all-to-all(bf16[8,8,2432]{2,1,0:T(8,128)(2,1)S(1)} %bitcast.8), channel_id=1, replica_groups=mesh['far'=4,'x'=4,'core'=2,'line'=8,'ring'=4] {'line'}, dimensions={0} | all-to-all | bytes 622592 | tf_op jit(solution)/shard_map/all_to_all | solution.py:121
  80.6 0.8 %finish.1 = (f32[8,1152]{1,0:T(8,128)}, f32[8,1152]{1,0:T(8,128)}, f32[8]{0:T(128)}) custom-call(bf16[64,2432]{1,0:T(8,128)(2,1)S(1)} %bitcast.9, bf16[8,1152]{1,0:T(8,128)(2,1)S(1)} %copy-done, bf16[8,1152]{1,0:T(8,128)(2,1)S(1)} %copy-done.1), custom_call_target="tpu_custom_call" | custom-call | tf_op jit(solution)/shard_map/finish/pallas_call | solution.py:162
  (2 shorter events, 0.0 us)
Async XLA Ops:
  1.4 34.3 %collective-permute-start.1 = (bf16[8,1152]{1,0:T(8,128)(2,1)S(1)}, bf16[8,1152]{1,0:T(8,128)(2,1)S(1)}, u32[]{:S(2)}, u32[]{:S(2)}) collective-permute-start(bf16[8,1152]{1,0:T(8,128)(2,1)S(1)} %get-tuple-element.3), channel_id=1, source_target_pairs={{64,128},{192,256},{320,384},{448,512},{576,640},{704,768},{832,89... | collective-permute-start | bytes 55304 | tf_op jit(solution)/shard_map/ppermute | solution.py:24
  4.8 30.9 %collective-permute-start = (bf16[8,1152]{1,0:T(8,128)(2,1)S(1)}, bf16[8,1152]{1,0:T(8,128)(2,1)S(1)}, u32[]{:S(2)}, u32[]{:S(2)}) collective-permute-start(bf16[8,1152]{1,0:T(8,128)(2,1)S(1)} %get-tuple-element.4), channel_id=1, source_target_pairs={{0,64},{128,192},{256,320},{384,448},{512,576},{640,704},{768,832}... | collective-permute-start | bytes 55304 | tf_op jit(solution)/shard_map/ppermute | solution.py:24
  30.5 5.2 %copy-start = (bf16[8,1152]{1,0:T(8,128)(2,1)S(1)}, bf16[8,1152]{1,0:T(8,128)(2,1)}, u32[]{:S(2)}) copy-start(bf16[8,1152]{1,0:T(8,128)(2,1)} %img_ref.7) | copy-start | bytes 55300
  30.5 5.2 %copy-start.1 = (bf16[8,1152]{1,0:T(8,128)(2,1)S(1)}, bf16[8,1152]{1,0:T(8,128)(2,1)}, u32[]{:S(2)}) copy-start(bf16[8,1152]{1,0:T(8,128)(2,1)} %txt_ref.7) | copy-start | bytes 55300
  30.5 22.5 %all-to-all-start = ((bf16[8,8,2304]{2,1,0:T(8,128)(2,1)}), bf16[8,8,2304]{2,1,0:T(8,128)(2,1)S(1)}, u32[]{:S(2)}, u32[]{:S(2)}) async-start(bf16[8,8,2304]{2,1,0:T(8,128)(2,1)} %bitcast.11), calls=%async_computation | async-start | bytes 589824 | tf_op jit(solution)/shard_map/all_to_all | solution.py:121
  35.7 3.2 %collective-permute-start.2 = (bf16[16,1152]{1,0:T(8,128)(2,1)S(1)}, bf16[16,1152]{1,0:T(8,128)(2,1)S(1)}, u32[]{:S(2)}, u32[]{:S(2)}) collective-permute-start(bf16[16,1152]{1,0:T(8,128)(2,1)S(1)} %mate.1), channel_id=1, source_target_pairs={{0,32},{32,0},{1,33},{33,1},{2,34},{34,2},{3,35},{35,3},{4,36},{36... | collective-permute-start | bytes 110600 | tf_op jit(solution)/shard_map/ppermute | solution.py:143

commit v8 on v7

--- a/solution.py
+++ b/solution.py
@@ -34,11 +34,14 @@
     return (grad - unit * jnp.sum(unit * grad, axis=-1, keepdims=True)) / norms
 
 
-def spread_kernel(img_ref, txt_ref, out_ref):
+def open_kernel(img_ref, txt_ref, near_ref, far_ref, line_ref):
+    even = (lax.axis_index("x") & 1) == 0
     width = img_ref.shape[1]
-    for ref, columns in ((img_ref, slice(0, width)), (txt_ref, slice(width, 2 * width))):
-        shard = ref[...].astype(jnp.float32)
-        out_ref[:, columns] = jnp.concatenate([shard] * LINE).astype(out_ref.dtype)
+    img, txt = img_ref[...].astype(jnp.float32), txt_ref[...].astype(jnp.float32)
+    near_ref[...] = jnp.where(even, txt, img).astype(near_ref.dtype)
+    far_ref[...] = jnp.where(even, img, txt).astype(far_ref.dtype)
+    line_ref[:, :width] = jnp.concatenate([img] * LINE).astype(line_ref.dtype)
+    line_ref[:, width:] = jnp.concatenate([txt] * LINE).astype(line_ref.dtype)
 
 
 def visitors(near, far):
@@ -120,16 +123,19 @@
         pieces = value.reshape(LINE, ROWS, value.shape[1])
         return lax.all_to_all(pieces, "line", 0, 0, tiled=True).reshape(value.shape)
 
-    even = (lax.axis_index("x") & 1) == 0
-    far = with_neighbour(jnp.where(even, images, texts), 1)
-    near = with_neighbour(jnp.where(even, texts, images), 0)
-    spread = pl.pallas_call(
-        spread_kernel,
-        out_shape=shape(LINE * ROWS, 2 * width, half),
+    near, far, spread = pl.pallas_call(
+        open_kernel,
+        out_shape=(
+            shape(ROWS, width, half),
+            shape(ROWS, width, half),
+            shape(LINE * ROWS, 2 * width, half),
+        ),
         in_specs=[VMEM] * 2,
-        out_specs=VMEM,
-        name="spread",
+        out_specs=(VMEM,) * 3,
+        name="open",
     )(images, texts)
+    far = with_neighbour(far, 1)
+    near = with_neighbour(near, 0)
     line = line_exchange(spread)
     mate = pl.pallas_call(
         mate_kernel,

time: 81.9 us -> 80.9 us (0.988)
  the two profiles are of different devices: /device:TPU:2 before, /device:TPU:8 now
where the time goes in v8:
time: 80.9 us; the launch traced here: 80.4 us
  blocking collectives  39.5 us (49%)
  starting transfers between devices  34.9 us (43%)
  Pallas kernels  3.16 us (4%)
  between operations  2.02 us (2%)
  waiting for transfers between devices  0.82 us (1%)
    ppermute x2, starting transfers between devices, with_neighbour(): return lax.ppermute(value, CHIPS, pairs + [(b, a) for a, b in pairs])  27.9 us
    all_to_all x1, blocking collectives, line_exchange(): return lax.all_to_all(pieces, 'line', 0, 0, tiled=True).reshape(value.shape)  26.3 us
    all_gather x1, blocking collectives, on_device(): ring = lax.all_gather(pack, 'ring', axis=0, tiled=True)  13.2 us
    all_to_all x1, starting transfers between devices, line_exchange(): return lax.all_to_all(pieces, 'line', 0, 0, tiled=True).reshape(value.shape)  5.04 us
    ppermute x1, starting transfers between devices, on_device(): mate = lax.ppermute(mate, 'core', [(0, 1), (1, 0)])  1.92 us
  transfers between devices with their start and end apart: 4, of which 1 were waited for; matrix products, arithmetic and copies ran while one was open for 0% of the time, Pallas kernels for 0%

profile of v8, /device:TPU:8, one launch (start us, length us, event | category | flops | bytes accessed | tf_op | source)
XLA Modules:
  0.0 80.4 jit_solution(2681875935666898894)
XLA Ops:
  0.6 1.5 %open.1 = (bf16[8,1152]{1,0:T(8,128)(2,1)}, bf16[8,1152]{1,0:T(8,128)(2,1)}, bf16[64,2304]{1,0:T(8,128)(2,1)}) custom-call(bf16[8,1152]{1,0:T(8,128)(2,1)} %img_ref.7, bf16[8,1152]{1,0:T(8,128)(2,1)} %txt_ref.7), custom_call_target="tpu_custom_call" | custom-call | tf_op jit(solution)/shard_map/open/pallas_call | solution.py:126
  2.1 3.4 %collective-permute-start = (bf16[8,1152]{1,0:T(8,128)(2,1)}, bf16[8,1152]{1,0:T(8,128)(2,1)S(1)}, u32[]{:S(2)}, u32[]{:S(2)}) collective-permute-start(bf16[8,1152]{1,0:T(8,128)(2,1)} %get-tuple-element.7), channel_id=1, source_target_pairs={{0,64},{128,192},{256,320},{384,448},{512,576},{640,704},{768,832}... | collective-permute-start | bytes 55304 | tf_op jit(solution)/shard_map/ppermute | solution.py:24
  5.5 24.5 %collective-permute-start.1 = (bf16[8,1152]{1,0:T(8,128)(2,1)}, bf16[8,1152]{1,0:T(8,128)(2,1)S(1)}, u32[]{:S(2)}, u32[]{:S(2)}) collective-permute-start(bf16[8,1152]{1,0:T(8,128)(2,1)} %get-tuple-element.8), channel_id=1, source_target_pairs={{64,128},{192,256},{320,384},{448,512},{576,640},{704,768},{832,89... | collective-permute-start | bytes 55304 | tf_op jit(solution)/shard_map/ppermute | solution.py:24
  30.0 0.0 copy-start
  30.1 0.0 copy-start.1
  30.1 5.0 %all-to-all-start = ((bf16[8,8,2304]{2,1,0:T(8,128)(2,1)}), bf16[8,8,2304]{2,1,0:T(8,128)(2,1)S(1)}, u32[]{:S(2)}, u32[]{:S(2)}) async-start(bf16[8,8,2304]{2,1,0:T(8,128)(2,1)} %bitcast.11), calls=%async_computation | async-start | bytes 589824 | tf_op jit(solution)/shard_map/all_to_all | solution.py:124
  35.1 0.0 collective-permute-done.near_ref
  35.1 0.0 collective-permute-done.1.far_ref
  35.1 0.0 copy-done
  35.1 0.0 copy-done.1
  35.2 1.9 %collective-permute-start.2 = (bf16[16,1152]{1,0:T(8,128)(2,1)S(1)}, bf16[16,1152]{1,0:T(8,128)(2,1)S(1)}, u32[]{:S(2)}, u32[]{:S(2)}) collective-permute-start(bf16[16,1152]{1,0:T(8,128)(2,1)S(1)} %mate.1), channel_id=1, source_target_pairs={{0,32},{32,0},{1,33},{33,1},{2,34},{34,2},{3,35},{35,3},{4,36},{36... | collective-permute-start | bytes 110600 | tf_op jit(solution)/shard_map/ppermute | solution.py:149
  38.4 0.0 collective-permute-done.2.mate_ref
  38.4 13.2 %all_gather.3.ring_ref = bf16[192,1152]{1,0:T(8,128)(2,1)S(1)} all-gather(bf16[48,1152]{1,0:T(8,128)(2,1)S(1)} %pack.1), channel_id=1, replica_groups=mesh['far'=4,'x'=4,'core'=2,'line'=8,'ring'=4] {'ring'}, dimensions={0}, use_global_device_ids=true | all-gather | bytes 552960 | tf_op jit(solution)/shard_map/all_gather | solution.py:158
  51.6 0.8 %all-to-all-done = bf16[8,8,2304]{2,1,0:T(8,128)(2,1)S(1)} async-done(((bf16[8,8,2304]{2,1,0:T(8,128)(2,1)}), bf16[8,8,2304]{2,1,0:T(8,128)(2,1)S(1)}, u32[]{:S(2)}, u32[]{:S(2)}) %all-to-all-start) | async-done | bytes 294944 | tf_op jit(solution)/shard_map/all_to_all | solution.py:124
  52.4 0.8 %score.1 = bf16[64,2432]{1,0:T(8,128)(2,1)S(1)} custom-call(f32[1]{0:T(128)} %bitcast.6.scale_ref, f32[1]{0:T(128)} %bitcast.7.bias_ref, bf16[64,2304]{1,0:T(8,128)(2,1)S(1)} %bitcast.10, bf16[192,1152]{1,0:T(8,128)(2,1)S(1)} %all_gather.3.ring_ref), custom_call_target="tpu_custom_call" | custom-call | tf_op jit(solution)/shard_map/score/pallas_call | solution.py:159
  53.2 26.3 %all_to_all.10 = bf16[8,8,2432]{2,1,0:T(8,128)(2,1)S(1)} all-to-all(bf16[8,8,2432]{2,1,0:T(8,128)(2,1)S(1)} %bitcast.8), channel_id=1, replica_groups=mesh['far'=4,'x'=4,'core'=2,'line'=8,'ring'=4] {'line'}, dimensions={0} | all-to-all | bytes 622592 | tf_op jit(solution)/shard_map/all_to_all | solution.py:124
  79.6 0.8 %finish.1 = (f32[8,1152]{1,0:T(8,128)}, f32[8,1152]{1,0:T(8,128)}, f32[8]{0:T(128)}) custom-call(bf16[64,2432]{1,0:T(8,128)(2,1)S(1)} %bitcast.9, bf16[8,1152]{1,0:T(8,128)(2,1)S(1)} %copy-done, bf16[8,1152]{1,0:T(8,128)(2,1)S(1)} %copy-done.1), custom_call_target="tpu_custom_call" | custom-call | tf_op jit(solution)/shard_map/finish/pallas_call | solution.py:168
  (2 shorter events, 0.0 us)
Async XLA Ops:
  2.1 33.0 %collective-permute-start = (bf16[8,1152]{1,0:T(8,128)(2,1)}, bf16[8,1152]{1,0:T(8,128)(2,1)S(1)}, u32[]{:S(2)}, u32[]{:S(2)}) collective-permute-start(bf16[8,1152]{1,0:T(8,128)(2,1)} %get-tuple-element.7), channel_id=1, source_target_pairs={{0,64},{128,192},{256,320},{384,448},{512,576},{640,704},{768,832}... | collective-permute-start | bytes 55304 | tf_op jit(solution)/shard_map/ppermute | solution.py:24
  5.5 29.6 %collective-permute-start.1 = (bf16[8,1152]{1,0:T(8,128)(2,1)}, bf16[8,1152]{1,0:T(8,128)(2,1)S(1)}, u32[]{:S(2)}, u32[]{:S(2)}) collective-permute-start(bf16[8,1152]{1,0:T(8,128)(2,1)} %get-tuple-element.8), channel_id=1, source_target_pairs={{64,128},{192,256},{320,384},{448,512},{576,640},{704,768},{832,89... | collective-permute-start | bytes 55304 | tf_op jit(solution)/shard_map/ppermute | solution.py:24
  30.0 5.1 %copy-start = (bf16[8,1152]{1,0:T(8,128)(2,1)S(1)}, bf16[8,1152]{1,0:T(8,128)(2,1)}, u32[]{:S(2)}) copy-start(bf16[8,1152]{1,0:T(8,128)(2,1)} %img_ref.7) | copy-start | bytes 55300
  30.1 5.1 %copy-start.1 = (bf16[8,1152]{1,0:T(8,128)(2,1)S(1)}, bf16[8,1152]{1,0:T(8,128)(2,1)}, u32[]{:S(2)}) copy-start(bf16[8,1152]{1,0:T(8,128)(2,1)} %txt_ref.7) | copy-start | bytes 55300
  30.1 22.3 %all-to-all-start = ((bf16[8,8,2304]{2,1,0:T(8,128)(2,1)}), bf16[8,8,2304]{2,1,0:T(8,128)(2,1)S(1)}, u32[]{:S(2)}, u32[]{:S(2)}) async-start(bf16[8,8,2304]{2,1,0:T(8,128)(2,1)} %bitcast.11), calls=%async_computation | async-start | bytes 589824 | tf_op jit(solution)/shard_map/all_to_all | solution.py:124
  35.2 3.2 %collective-permute-start.2 = (bf16[16,1152]{1,0:T(8,128)(2,1)S(1)}, bf16[16,1152]{1,0:T(8,128)(2,1)S(1)}, u32[]{:S(2)}, u32[]{:S(2)}) collective-permute-start(bf16[16,1152]{1,0:T(8,128)(2,1)S(1)} %mate.1), channel_id=1, source_target_pairs={{0,32},{32,0},{1,33},{33,1},{2,34},{34,2},{3,35},{35,3},{4,36},{36... | collective-permute-start | bytes 110600 | tf_op jit(solution)/shard_map/ppermute | solution.py:149

commit v9 on v8

--- a/solution.py
+++ b/solution.py
@@ -13,6 +13,7 @@
 CHIPS = ("far", "x")
 SHARE = ROUNDS * ROWS
 LANES = 128
+ORDER = (4, 5, 6, 7, 0, 1, 2, 3)
 SMEM = pl.BlockSpec(memory_space=pltpu.SMEM)
 VMEM = pl.BlockSpec(memory_space=pltpu.VMEM)
 ROOM = pltpu.CompilerParams(vmem_limit_bytes=8 * 2**20)
@@ -68,6 +69,7 @@
 def score_kernel(scale_ref, bias_ref, line_ref, ring_ref, out_ref):
     scale, bias = scale_ref[0], bias_ref[0]
     line, ring = lax.axis_index("line"), lax.axis_index("ring")
+    place = sum(jnp.where(line == at, slot, 0) for slot, at in enumerate(ORDER))
     width = ring_ref.shape[1]
     around = normalize(ring_ref[...])[0].reshape(RING, 2, SHARE, width)
 
@@ -78,7 +80,7 @@
             ours, others, (((1,), (1,)), ((), ())), preferred_element_type=jnp.float32
         )
         logit = scale * dots + bias
-        row = lax.broadcasted_iota(jnp.int32, logit.shape, 0) - line * ROWS
+        row = lax.broadcasted_iota(jnp.int32, logit.shape, 0) - place * ROWS
         column = lax.broadcasted_iota(jnp.int32, logit.shape, 1) - ring * SHARE
         own = (row == column) & (row >= 0) & (row < ROWS)
         signed = jnp.where(own, -logit, logit)
@@ -121,7 +123,9 @@
 
     def line_exchange(value):
         pieces = value.reshape(LINE, ROWS, value.shape[1])
-        return lax.all_to_all(pieces, "line", 0, 0, tiled=True).reshape(value.shape)
+        return lax.all_to_all(
+            pieces, "line", 0, 0, tiled=True, axis_index_groups=[list(ORDER)]
+        ).reshape(value.shape)
 
     near, far, spread = pl.pallas_call(
         open_kernel,

time: 80.9 us -> 75 us (0.927)
  blocking collectives: 39.5 us -> 32.3 us
  starting transfers between devices: 34.9 us -> 37.1 us
  waiting for transfers between devices: 0.82 us -> 0.01 us
    all_to_all x1, blocking collectives: 26.3 us -> 19.3 us  [line_exchange(): lax.all_to_all(pieces, 'line', 0, 0, tiled=True, axis_index_groups=[list(...]
    all_to_all x1, starting transfers between devices: 5.04 us -> 7.22 us  [line_exchange(): lax.all_to_all(pieces, 'line', 0, 0, tiled=True, axis_index_groups=[list(...]
    all_to_all x1, waiting for transfers between devices: 0.81 us -> 0.01 us  [line_exchange(): lax.all_to_all(pieces, 'line', 0, 0, tiled=True, axis_index_groups=[list(...]
  transfers between devices with their start and end apart: 4 -> 4, of which waited for: 1 -> 0; matrix products, arithmetic and copies ran while one was open for 0% -> 0% of each run, Pallas kernels for 0% -> 0%
where the time goes in v9:
time: 75 us; the launch traced here: 74.5 us
  starting transfers between devices  37.1 us (49%)
  blocking collectives  32.3 us (43%)
  Pallas kernels  3.16 us (4%)
  between operations  2.02 us (3%)
    ppermute x2, starting transfers between devices, with_neighbour(): return lax.ppermute(value, CHIPS, pairs + [(b, a) for a, b in pairs])  27.9 us
    all_to_all x1, blocking collectives, line_exchange(): lax.all_to_all(pieces, 'line', 0, 0, tiled=True, axis_index_groups=[list(...  19.3 us
    all_gather x1, blocking collectives, on_device(): ring = lax.all_gather(pack, 'ring', axis=0, tiled=True)  13 us
    all_to_all x1, starting transfers between devices, line_exchange(): lax.all_to_all(pieces, 'line', 0, 0, tiled=True, axis_index_groups=[list(...  7.22 us
    ppermute x1, starting transfers between devices, on_device(): mate = lax.ppermute(mate, 'core', [(0, 1), (1, 0)])  1.92 us
  transfers between devices with their start and end apart: 4, of which 0 were waited for; matrix products, arithmetic and copies ran while one was open for 0% of the time, Pallas kernels for 0%

profile of v9, /device:TPU:8, one launch (start us, length us, event | category | flops | bytes accessed | tf_op | source)
XLA Modules:
  0.0 74.5 jit_solution(3880393977794804623)
XLA Ops:
  0.6 1.5 %open.1 = (bf16[8,1152]{1,0:T(8,128)(2,1)}, bf16[8,1152]{1,0:T(8,128)(2,1)}, bf16[64,2304]{1,0:T(8,128)(2,1)}) custom-call(bf16[8,1152]{1,0:T(8,128)(2,1)} %img_ref.7, bf16[8,1152]{1,0:T(8,128)(2,1)} %txt_ref.7), custom_call_target="tpu_custom_call" | custom-call | tf_op jit(solution)/shard_map/open/pallas_call | solution.py:130
  2.1 3.4 %collective-permute-start = (bf16[8,1152]{1,0:T(8,128)(2,1)}, bf16[8,1152]{1,0:T(8,128)(2,1)S(1)}, u32[]{:S(2)}, u32[]{:S(2)}) collective-permute-start(bf16[8,1152]{1,0:T(8,128)(2,1)} %get-tuple-element.7), channel_id=1, source_target_pairs={{0,64},{128,192},{256,320},{384,448},{512,576},{640,704},{768,832}... | collective-permute-start | bytes 55304 | tf_op jit(solution)/shard_map/ppermute | solution.py:25
  5.5 24.5 %collective-permute-start.1 = (bf16[8,1152]{1,0:T(8,128)(2,1)}, bf16[8,1152]{1,0:T(8,128)(2,1)S(1)}, u32[]{:S(2)}, u32[]{:S(2)}) collective-permute-start(bf16[8,1152]{1,0:T(8,128)(2,1)} %get-tuple-element.8), channel_id=1, source_target_pairs={{64,128},{192,256},{320,384},{448,512},{576,640},{704,768},{832,89... | collective-permute-start | bytes 55304 | tf_op jit(solution)/shard_map/ppermute | solution.py:25
  30.0 0.0 copy-start
  30.1 0.0 copy-start.1
  30.1 7.2 %all-to-all-start = ((bf16[8,8,2304]{2,1,0:T(8,128)(2,1)}), bf16[8,8,2304]{2,1,0:T(8,128)(2,1)S(1)}, u32[]{:S(2)}, u32[]{:S(2)}) async-start(bf16[8,8,2304]{2,1,0:T(8,128)(2,1)} %bitcast.11), calls=%async_computation | async-start | bytes 589824 | tf_op jit(solution)/shard_map/all_to_all | solution.py:126
  37.3 0.0 collective-permute-done.near_ref
  37.3 0.0 collective-permute-done.1.far_ref
  37.3 0.0 copy-done
  37.3 0.0 copy-done.1
  37.3 1.9 %collective-permute-start.2 = (bf16[16,1152]{1,0:T(8,128)(2,1)S(1)}, bf16[16,1152]{1,0:T(8,128)(2,1)S(1)}, u32[]{:S(2)}, u32[]{:S(2)}) collective-permute-start(bf16[16,1152]{1,0:T(8,128)(2,1)S(1)} %mate.1), channel_id=1, source_target_pairs={{0,32},{32,0},{1,33},{33,1},{2,34},{34,2},{3,35},{35,3},{4,36},{36... | collective-permute-start | bytes 110600 | tf_op jit(solution)/shard_map/ppermute | solution.py:153
  40.6 0.0 collective-permute-done.2.mate_ref
  40.6 13.0 %all_gather.3.ring_ref = bf16[192,1152]{1,0:T(8,128)(2,1)S(1)} all-gather(bf16[48,1152]{1,0:T(8,128)(2,1)S(1)} %pack.1), channel_id=1, replica_groups=mesh['far'=4,'x'=4,'core'=2,'line'=8,'ring'=4] {'ring'}, dimensions={0}, use_global_device_ids=true | all-gather | bytes 552960 | tf_op jit(solution)/shard_map/all_gather | solution.py:162
  53.6 0.0 all-to-all-done
  53.6 0.8 %score.1 = bf16[64,2432]{1,0:T(8,128)(2,1)S(1)} custom-call(f32[1]{0:T(128)} %bitcast.6.scale_ref, f32[1]{0:T(128)} %bitcast.7.bias_ref, bf16[64,2304]{1,0:T(8,128)(2,1)S(1)} %bitcast.10, bf16[192,1152]{1,0:T(8,128)(2,1)S(1)} %all_gather.3.ring_ref), custom_call_target="tpu_custom_call" | custom-call | tf_op jit(solution)/shard_map/score/pallas_call | solution.py:163
  54.4 19.3 %all_to_all.10 = bf16[8,8,2432]{2,1,0:T(8,128)(2,1)S(1)} all-to-all(bf16[8,8,2432]{2,1,0:T(8,128)(2,1)S(1)} %bitcast.8), channel_id=1, replica_groups={{16,20,24,28,0,4,8,12},{17,21,25,29,1,5,9,13},{18,22,26,30,2,6,10,14},{..., dimensions={0} | all-to-all | bytes 622592 | tf_op jit(solution)/shard_map/all_to_all | solution.py:126
  73.7 0.8 %finish.1 = (f32[8,1152]{1,0:T(8,128)}, f32[8,1152]{1,0:T(8,128)}, f32[8]{0:T(128)}) custom-call(bf16[64,2432]{1,0:T(8,128)(2,1)S(1)} %bitcast.9, bf16[8,1152]{1,0:T(8,128)(2,1)S(1)} %copy-done, bf16[8,1152]{1,0:T(8,128)(2,1)S(1)} %copy-done.1), custom_call_target="tpu_custom_call" | custom-call | tf_op jit(solution)/shard_map/finish/pallas_call | solution.py:172
  (2 shorter events, 0.0 us)
Async XLA Ops:
  2.1 35.2 %collective-permute-start = (bf16[8,1152]{1,0:T(8,128)(2,1)}, bf16[8,1152]{1,0:T(8,128)(2,1)S(1)}, u32[]{:S(2)}, u32[]{:S(2)}) collective-permute-start(bf16[8,1152]{1,0:T(8,128)(2,1)} %get-tuple-element.7), channel_id=1, source_target_pairs={{0,64},{128,192},{256,320},{384,448},{512,576},{640,704},{768,832}... | collective-permute-start | bytes 55304 | tf_op jit(solution)/shard_map/ppermute | solution.py:25
  5.5 31.8 %collective-permute-start.1 = (bf16[8,1152]{1,0:T(8,128)(2,1)}, bf16[8,1152]{1,0:T(8,128)(2,1)S(1)}, u32[]{:S(2)}, u32[]{:S(2)}) collective-permute-start(bf16[8,1152]{1,0:T(8,128)(2,1)} %get-tuple-element.8), channel_id=1, source_target_pairs={{64,128},{192,256},{320,384},{448,512},{576,640},{704,768},{832,89... | collective-permute-start | bytes 55304 | tf_op jit(solution)/shard_map/ppermute | solution.py:25
  30.0 7.3 %copy-start = (bf16[8,1152]{1,0:T(8,128)(2,1)S(1)}, bf16[8,1152]{1,0:T(8,128)(2,1)}, u32[]{:S(2)}) copy-start(bf16[8,1152]{1,0:T(8,128)(2,1)} %img_ref.7) | copy-start | bytes 55300
  30.1 7.3 %copy-start.1 = (bf16[8,1152]{1,0:T(8,128)(2,1)S(1)}, bf16[8,1152]{1,0:T(8,128)(2,1)}, u32[]{:S(2)}) copy-start(bf16[8,1152]{1,0:T(8,128)(2,1)} %txt_ref.7) | copy-start | bytes 55300
  30.1 23.5 %all-to-all-start = ((bf16[8,8,2304]{2,1,0:T(8,128)(2,1)}), bf16[8,8,2304]{2,1,0:T(8,128)(2,1)S(1)}, u32[]{:S(2)}, u32[]{:S(2)}) async-start(bf16[8,8,2304]{2,1,0:T(8,128)(2,1)} %bitcast.11), calls=%async_computation | async-start | bytes 589824 | tf_op jit(solution)/shard_map/all_to_all | solution.py:126
  37.3 3.2 %collective-permute-start.2 = (bf16[16,1152]{1,0:T(8,128)(2,1)S(1)}, bf16[16,1152]{1,0:T(8,128)(2,1)S(1)}, u32[]{:S(2)}, u32[]{:S(2)}) collective-permute-start(bf16[16,1152]{1,0:T(8,128)(2,1)S(1)} %mate.1), channel_id=1, source_target_pairs={{0,32},{32,0},{1,33},{33,1},{2,34},{34,2},{3,35},{35,3},{4,36},{36... | collective-permute-start | bytes 110600 | tf_op jit(solution)/shard_map/ppermute | solution.py:153

commit v10 on v9

--- a/solution.py
+++ b/solution.py
@@ -13,7 +13,8 @@
 CHIPS = ("far", "x")
 SHARE = ROUNDS * ROWS
 LANES = 128
-ORDER = (4, 5, 6, 7, 0, 1, 2, 3)
+OUT = (3, 4, 5, 6, 7, 0, 1, 2)
+BACK = (4, 5, 6, 7, 0, 1, 2, 3)
 SMEM = pl.BlockSpec(memory_space=pltpu.SMEM)
 VMEM = pl.BlockSpec(memory_space=pltpu.VMEM)
 ROOM = pltpu.CompilerParams(vmem_limit_bytes=8 * 2**20)
@@ -69,12 +70,13 @@
 def score_kernel(scale_ref, bias_ref, line_ref, ring_ref, out_ref):
     scale, bias = scale_ref[0], bias_ref[0]
     line, ring = lax.axis_index("line"), lax.axis_index("ring")
-    place = sum(jnp.where(line == at, slot, 0) for slot, at in enumerate(ORDER))
+    place = sum(jnp.where(line == at, slot, 0) for slot, at in enumerate(BACK))
     width = ring_ref.shape[1]
     around = normalize(ring_ref[...])[0].reshape(RING, 2, SHARE, width)
 
     def against(ours, others):
-        ours = normalize(ours)[0].astype(jnp.bfloat16)
+        ours = normalize(ours)[0].reshape(LINE, ROWS, width)
+        ours = jnp.concatenate([ours[OUT.index(at)] for at in BACK]).astype(jnp.bfloat16)
         others = others.reshape(RING * SHARE, width).astype(jnp.bfloat16)
         dots = lax.dot_general(
             ours, others, (((1,), (1,)), ((), ())), preferred_element_type=jnp.float32
@@ -121,10 +123,10 @@
     def shape(rows, columns, kind):
         return jax.ShapeDtypeStruct((rows, columns), kind)
 
-    def line_exchange(value):
+    def line_exchange(value, order):
         pieces = value.reshape(LINE, ROWS, value.shape[1])
         return lax.all_to_all(
-            pieces, "line", 0, 0, tiled=True, axis_index_groups=[list(ORDER)]
+            pieces, "line", 0, 0, tiled=True, axis_index_groups=[list(order)]
         ).reshape(value.shape)
 
     near, far, spread = pl.pallas_call(
@@ -140,7 +142,7 @@
     )(images, texts)
     far = with_neighbour(far, 1)
     near = with_neighbour(near, 0)
-    line = line_exchange(spread)
+    line = line_exchange(spread, OUT)
     mate = pl.pallas_call(
         mate_kernel,
         out_shape=shape(2 * ROWS, width, half),
@@ -168,7 +170,7 @@
         compiler_params=ROOM,
         name="score",
     )(scale.reshape(1), bias.reshape(1), line, ring)
-    parts = line_exchange(parts)
+    parts = line_exchange(parts, BACK)
     return pl.pallas_call(
         finish_kernel,
         out_shape=(

time: 75 us -> 73.6 us (0.981)
  starting transfers between devices: 37.1 us -> 35.4 us
    all_to_all x1, starting transfers between devices: 7.22 us -> 5.6 us  [line_exchange(): lax.all_to_all(pieces, 'line', 0, 0, tiled=True, axis_index_groups=[list(...]
where the time goes in v10:
time: 73.6 us; the launch traced here: 73.2 us
  starting transfers between devices  35.4 us (48%)
  blocking collectives  32.6 us (44%)
  Pallas kernels  3.16 us (4%)
  between operations  2.02 us (3%)
    ppermute x2, starting transfers between devices, with_neighbour(): return lax.ppermute(value, CHIPS, pairs + [(b, a) for a, b in pairs])  27.9 us
    all_to_all x1, blocking collectives, line_exchange(): lax.all_to_all(pieces, 'line', 0, 0, tiled=True, axis_index_groups=[list(...  19.6 us
    all_gather x1, blocking collectives, on_device(): ring = lax.all_gather(pack, 'ring', axis=0, tiled=True)  13 us
    all_to_all x1, starting transfers between devices, line_exchange(): lax.all_to_all(pieces, 'line', 0, 0, tiled=True, axis_index_groups=[list(...  5.6 us
    ppermute x1, starting transfers between devices, on_device(): mate = lax.ppermute(mate, 'core', [(0, 1), (1, 0)])  1.92 us
    pallas_call x1, Pallas kernels, on_device(): pl.pallas_call(open_kernel, out_shape=(shape(ROWS, width, half), shape(RO...  1.48 us
  transfers between devices with their start and end apart: 4, of which 0 were waited for; matrix products, arithmetic and copies ran while one was open for 0% of the time, Pallas kernels for 0%

profile of v10, /device:TPU:8, one launch (start us, length us, event | category | flops | bytes accessed | tf_op | source)
XLA Modules:
  0.0 73.2 jit_solution(4153704188581978726)
XLA Ops:
  0.6 1.5 %open.1 = (bf16[8,1152]{1,0:T(8,128)(2,1)}, bf16[8,1152]{1,0:T(8,128)(2,1)}, bf16[64,2304]{1,0:T(8,128)(2,1)}) custom-call(bf16[8,1152]{1,0:T(8,128)(2,1)} %img_ref.7, bf16[8,1152]{1,0:T(8,128)(2,1)} %txt_ref.7), custom_call_target="tpu_custom_call" | custom-call | tf_op jit(solution)/shard_map/open/pallas_call | solution.py:132
  2.1 3.4 %collective-permute-start = (bf16[8,1152]{1,0:T(8,128)(2,1)}, bf16[8,1152]{1,0:T(8,128)(2,1)S(1)}, u32[]{:S(2)}, u32[]{:S(2)}) collective-permute-start(bf16[8,1152]{1,0:T(8,128)(2,1)} %get-tuple-element.7), channel_id=1, source_target_pairs={{0,64},{128,192},{256,320},{384,448},{512,576},{640,704},{768,832}... | collective-permute-start | bytes 55304 | tf_op jit(solution)/shard_map/ppermute | solution.py:26
  5.5 24.5 %collective-permute-start.1 = (bf16[8,1152]{1,0:T(8,128)(2,1)}, bf16[8,1152]{1,0:T(8,128)(2,1)S(1)}, u32[]{:S(2)}, u32[]{:S(2)}) collective-permute-start(bf16[8,1152]{1,0:T(8,128)(2,1)} %get-tuple-element.8), channel_id=1, source_target_pairs={{64,128},{192,256},{320,384},{448,512},{576,640},{704,768},{832,89... | collective-permute-start | bytes 55304 | tf_op jit(solution)/shard_map/ppermute | solution.py:26
  30.0 0.0 copy-start
  30.1 0.0 copy-start.1
  30.1 5.6 %all-to-all-start = ((bf16[8,8,2304]{2,1,0:T(8,128)(2,1)}), bf16[8,8,2304]{2,1,0:T(8,128)(2,1)S(1)}, u32[]{:S(2)}, u32[]{:S(2)}) async-start(bf16[8,8,2304]{2,1,0:T(8,128)(2,1)} %bitcast.11), calls=%async_computation | async-start | bytes 589824 | tf_op jit(solution)/shard_map/all_to_all | solution.py:128
  35.7 0.0 collective-permute-done.near_ref
  35.7 0.0 collective-permute-done.1.far_ref
  35.7 0.0 copy-done
  35.7 0.0 copy-done.1
  35.7 1.9 %collective-permute-start.2 = (bf16[16,1152]{1,0:T(8,128)(2,1)S(1)}, bf16[16,1152]{1,0:T(8,128)(2,1)S(1)}, u32[]{:S(2)}, u32[]{:S(2)}) collective-permute-start(bf16[16,1152]{1,0:T(8,128)(2,1)S(1)} %mate.1), channel_id=1, source_target_pairs={{0,32},{32,0},{1,33},{33,1},{2,34},{34,2},{3,35},{35,3},{4,36},{36... | collective-permute-start | bytes 110600 | tf_op jit(solution)/shard_map/ppermute | solution.py:155
  38.9 0.0 collective-permute-done.2.mate_ref
  39.0 13.0 %all_gather.3.ring_ref = bf16[192,1152]{1,0:T(8,128)(2,1)S(1)} all-gather(bf16[48,1152]{1,0:T(8,128)(2,1)S(1)} %pack.1), channel_id=1, replica_groups=mesh['far'=4,'x'=4,'core'=2,'line'=8,'ring'=4] {'ring'}, dimensions={0}, use_global_device_ids=true | all-gather | bytes 552960 | tf_op jit(solution)/shard_map/all_gather | solution.py:164
  52.0 0.0 all-to-all-done
  52.0 0.8 %score.1 = bf16[64,2432]{1,0:T(8,128)(2,1)S(1)} custom-call(f32[1]{0:T(128)} %bitcast.6.scale_ref, f32[1]{0:T(128)} %bitcast.7.bias_ref, bf16[64,2304]{1,0:T(8,128)(2,1)S(1)} %bitcast.10, bf16[192,1152]{1,0:T(8,128)(2,1)S(1)} %all_gather.3.ring_ref), custom_call_target="tpu_custom_call" | custom-call | tf_op jit(solution)/shard_map/score/pallas_call | solution.py:165
  52.8 19.6 %all_to_all.10 = bf16[8,8,2432]{2,1,0:T(8,128)(2,1)S(1)} all-to-all(bf16[8,8,2432]{2,1,0:T(8,128)(2,1)S(1)} %bitcast.8), channel_id=1, replica_groups={{16,20,24,28,0,4,8,12},{17,21,25,29,1,5,9,13},{18,22,26,30,2,6,10,14},{..., dimensions={0} | all-to-all | bytes 622592 | tf_op jit(solution)/shard_map/all_to_all | solution.py:128
  72.4 0.8 %finish.1 = (f32[8,1152]{1,0:T(8,128)}, f32[8,1152]{1,0:T(8,128)}, f32[8]{0:T(128)}) custom-call(bf16[64,2432]{1,0:T(8,128)(2,1)S(1)} %bitcast.9, bf16[8,1152]{1,0:T(8,128)(2,1)S(1)} %copy-done, bf16[8,1152]{1,0:T(8,128)(2,1)S(1)} %copy-done.1), custom_call_target="tpu_custom_call" | custom-call | tf_op jit(solution)/shard_map/finish/pallas_call | solution.py:174
  (2 shorter events, 0.0 us)
Async XLA Ops:
  2.1 33.6 %collective-permute-start = (bf16[8,1152]{1,0:T(8,128)(2,1)}, bf16[8,1152]{1,0:T(8,128)(2,1)S(1)}, u32[]{:S(2)}, u32[]{:S(2)}) collective-permute-start(bf16[8,1152]{1,0:T(8,128)(2,1)} %get-tuple-element.7), channel_id=1, source_target_pairs={{0,64},{128,192},{256,320},{384,448},{512,576},{640,704},{768,832}... | collective-permute-start | bytes 55304 | tf_op jit(solution)/shard_map/ppermute | solution.py:26
  5.5 30.2 %collective-permute-start.1 = (bf16[8,1152]{1,0:T(8,128)(2,1)}, bf16[8,1152]{1,0:T(8,128)(2,1)S(1)}, u32[]{:S(2)}, u32[]{:S(2)}) collective-permute-start(bf16[8,1152]{1,0:T(8,128)(2,1)} %get-tuple-element.8), channel_id=1, source_target_pairs={{64,128},{192,256},{320,384},{448,512},{576,640},{704,768},{832,89... | collective-permute-start | bytes 55304 | tf_op jit(solution)/shard_map/ppermute | solution.py:26
  30.0 5.6 %copy-start = (bf16[8,1152]{1,0:T(8,128)(2,1)S(1)}, bf16[8,1152]{1,0:T(8,128)(2,1)}, u32[]{:S(2)}) copy-start(bf16[8,1152]{1,0:T(8,128)(2,1)} %img_ref.7) | copy-start | bytes 55300
  30.1 5.6 %copy-start.1 = (bf16[8,1152]{1,0:T(8,128)(2,1)S(1)}, bf16[8,1152]{1,0:T(8,128)(2,1)}, u32[]{:S(2)}) copy-start(bf16[8,1152]{1,0:T(8,128)(2,1)} %txt_ref.7) | copy-start | bytes 55300
  30.1 21.9 %all-to-all-start = ((bf16[8,8,2304]{2,1,0:T(8,128)(2,1)}), bf16[8,8,2304]{2,1,0:T(8,128)(2,1)S(1)}, u32[]{:S(2)}, u32[]{:S(2)}) async-start(bf16[8,8,2304]{2,1,0:T(8,128)(2,1)} %bitcast.11), calls=%async_computation | async-start | bytes 589824 | tf_op jit(solution)/shard_map/all_to_all | solution.py:128
  35.7 3.2 %collective-permute-start.2 = (bf16[16,1152]{1,0:T(8,128)(2,1)S(1)}, bf16[16,1152]{1,0:T(8,128)(2,1)S(1)}, u32[]{:S(2)}, u32[]{:S(2)}) collective-permute-start(bf16[16,1152]{1,0:T(8,128)(2,1)S(1)} %mate.1), channel_id=1, source_target_pairs={{0,32},{32,0},{1,33},{33,1},{2,34},{34,2},{3,35},{35,3},{4,36},{36... | collective-permute-start | bytes 110600 | tf_op jit(solution)/shard_map/ppermute | solution.py:155

commit v11 on v10

--- a/solution.py
+++ b/solution.py
@@ -13,7 +13,7 @@
 CHIPS = ("far", "x")
 SHARE = ROUNDS * ROWS
 LANES = 128
-OUT = (3, 4, 5, 6, 7, 0, 1, 2)
+OUT = (2, 3, 4, 5, 6, 7, 0, 1)
 BACK = (4, 5, 6, 7, 0, 1, 2, 3)
 SMEM = pl.BlockSpec(memory_space=pltpu.SMEM)
 VMEM = pl.BlockSpec(memory_space=pltpu.VMEM)

time: 73.6 us -> 74.3 us (level)
  no operation moved by 1% of the time
where the time goes in v11:
time: 74.3 us; the launch traced here: 73.9 us
  starting transfers between devices  35.4 us (48%)
  blocking collectives  33.3 us (45%)
  Pallas kernels  3.16 us (4%)
  between operations  2.02 us (3%)
    ppermute x2, starting transfers between devices, with_neighbour(): return lax.ppermute(value, CHIPS, pairs + [(b, a) for a, b in pairs])  27.9 us
    all_to_all x1, blocking collectives, line_exchange(): lax.all_to_all(pieces, 'line', 0, 0, tiled=True, axis_index_groups=[list(...  20.3 us
    all_gather x1, blocking collectives, on_device(): ring = lax.all_gather(pack, 'ring', axis=0, tiled=True)  13 us
    all_to_all x1, starting transfers between devices, line_exchange(): lax.all_to_all(pieces, 'line', 0, 0, tiled=True, axis_index_groups=[list(...  5.6 us
    ppermute x1, starting transfers between devices, on_device(): mate = lax.ppermute(mate, 'core', [(0, 1), (1, 0)])  1.92 us
  transfers between devices with their start and end apart: 4, of which 0 were waited for; matrix products, arithmetic and copies ran while one was open for 0% of the time, Pallas kernels for 0%

profile of v11, /device:TPU:8, one launch (start us, length us, event | category | flops | bytes accessed | tf_op | source)
XLA Modules:
  0.0 73.9 jit_solution(12732938886827141008)
XLA Ops:
  0.6 1.5 %open.1 = (bf16[8,1152]{1,0:T(8,128)(2,1)}, bf16[8,1152]{1,0:T(8,128)(2,1)}, bf16[64,2304]{1,0:T(8,128)(2,1)}) custom-call(bf16[8,1152]{1,0:T(8,128)(2,1)} %img_ref.7, bf16[8,1152]{1,0:T(8,128)(2,1)} %txt_ref.7), custom_call_target="tpu_custom_call" | custom-call | tf_op jit(solution)/shard_map/open/pallas_call | solution.py:132
  2.1 3.4 %collective-permute-start = (bf16[8,1152]{1,0:T(8,128)(2,1)}, bf16[8,1152]{1,0:T(8,128)(2,1)S(1)}, u32[]{:S(2)}, u32[]{:S(2)}) collective-permute-start(bf16[8,1152]{1,0:T(8,128)(2,1)} %get-tuple-element.7), channel_id=1, source_target_pairs={{0,64},{128,192},{256,320},{384,448},{512,576},{640,704},{768,832}... | collective-permute-start | bytes 55304 | tf_op jit(solution)/shard_map/ppermute | solution.py:26
  5.5 24.5 %collective-permute-start.1 = (bf16[8,1152]{1,0:T(8,128)(2,1)}, bf16[8,1152]{1,0:T(8,128)(2,1)S(1)}, u32[]{:S(2)}, u32[]{:S(2)}) collective-permute-start(bf16[8,1152]{1,0:T(8,128)(2,1)} %get-tuple-element.8), channel_id=1, source_target_pairs={{64,128},{192,256},{320,384},{448,512},{576,640},{704,768},{832,89... | collective-permute-start | bytes 55304 | tf_op jit(solution)/shard_map/ppermute | solution.py:26
  30.0 0.0 copy-start
  30.1 0.0 copy-start.1
  30.1 5.6 %all-to-all-start = ((bf16[8,8,2304]{2,1,0:T(8,128)(2,1)}), bf16[8,8,2304]{2,1,0:T(8,128)(2,1)S(1)}, u32[]{:S(2)}, u32[]{:S(2)}) async-start(bf16[8,8,2304]{2,1,0:T(8,128)(2,1)} %bitcast.11), calls=%async_computation | async-start | bytes 589824 | tf_op jit(solution)/shard_map/all_to_all | solution.py:128
  35.7 0.0 collective-permute-done.near_ref
  35.7 0.0 collective-permute-done.1.far_ref
  35.7 0.0 copy-done
  35.7 0.0 copy-done.1
  35.7 1.9 %collective-permute-start.2 = (bf16[16,1152]{1,0:T(8,128)(2,1)S(1)}, bf16[16,1152]{1,0:T(8,128)(2,1)S(1)}, u32[]{:S(2)}, u32[]{:S(2)}) collective-permute-start(bf16[16,1152]{1,0:T(8,128)(2,1)S(1)} %mate.1), channel_id=1, source_target_pairs={{0,32},{32,0},{1,33},{33,1},{2,34},{34,2},{3,35},{35,3},{4,36},{36... | collective-permute-start | bytes 110600 | tf_op jit(solution)/shard_map/ppermute | solution.py:155
  38.9 0.0 collective-permute-done.2.mate_ref
  39.0 13.0 %all_gather.3.ring_ref = bf16[192,1152]{1,0:T(8,128)(2,1)S(1)} all-gather(bf16[48,1152]{1,0:T(8,128)(2,1)S(1)} %pack.1), channel_id=1, replica_groups=mesh['far'=4,'x'=4,'core'=2,'line'=8,'ring'=4] {'ring'}, dimensions={0}, use_global_device_ids=true | all-gather | bytes 552960 | tf_op jit(solution)/shard_map/all_gather | solution.py:164
  52.0 0.0 all-to-all-done
  52.0 0.8 %score.1 = bf16[64,2432]{1,0:T(8,128)(2,1)S(1)} custom-call(f32[1]{0:T(128)} %bitcast.6.scale_ref, f32[1]{0:T(128)} %bitcast.7.bias_ref, bf16[64,2304]{1,0:T(8,128)(2,1)S(1)} %bitcast.10, bf16[192,1152]{1,0:T(8,128)(2,1)S(1)} %all_gather.3.ring_ref), custom_call_target="tpu_custom_call" | custom-call | tf_op jit(solution)/shard_map/score/pallas_call | solution.py:165
  52.8 20.3 %all_to_all.10 = bf16[8,8,2432]{2,1,0:T(8,128)(2,1)S(1)} all-to-all(bf16[8,8,2432]{2,1,0:T(8,128)(2,1)S(1)} %bitcast.8), channel_id=1, replica_groups={{16,20,24,28,0,4,8,12},{17,21,25,29,1,5,9,13},{18,22,26,30,2,6,10,14},{..., dimensions={0} | all-to-all | bytes 622592 | tf_op jit(solution)/shard_map/all_to_all | solution.py:128
  73.1 0.8 %finish.1 = (f32[8,1152]{1,0:T(8,128)}, f32[8,1152]{1,0:T(8,128)}, f32[8]{0:T(128)}) custom-call(bf16[64,2432]{1,0:T(8,128)(2,1)S(1)} %bitcast.9, bf16[8,1152]{1,0:T(8,128)(2,1)S(1)} %copy-done, bf16[8,1152]{1,0:T(8,128)(2,1)S(1)} %copy-done.1), custom_call_target="tpu_custom_call" | custom-call | tf_op jit(solution)/shard_map/finish/pallas_call | solution.py:174
  (2 shorter events, 0.0 us)
Async XLA Ops:
  2.1 33.6 %collective-permute-start = (bf16[8,1152]{1,0:T(8,128)(2,1)}, bf16[8,1152]{1,0:T(8,128)(2,1)S(1)}, u32[]{:S(2)}, u32[]{:S(2)}) collective-permute-start(bf16[8,1152]{1,0:T(8,128)(2,1)} %get-tuple-element.7), channel_id=1, source_target_pairs={{0,64},{128,192},{256,320},{384,448},{512,576},{640,704},{768,832}... | collective-permute-start | bytes 55304 | tf_op jit(solution)/shard_map/ppermute | solution.py:26
  5.5 30.2 %collective-permute-start.1 = (bf16[8,1152]{1,0:T(8,128)(2,1)}, bf16[8,1152]{1,0:T(8,128)(2,1)S(1)}, u32[]{:S(2)}, u32[]{:S(2)}) collective-permute-start(bf16[8,1152]{1,0:T(8,128)(2,1)} %get-tuple-element.8), channel_id=1, source_target_pairs={{64,128},{192,256},{320,384},{448,512},{576,640},{704,768},{832,89... | collective-permute-start | bytes 55304 | tf_op jit(solution)/shard_map/ppermute | solution.py:26
  30.0 5.6 %copy-start = (bf16[8,1152]{1,0:T(8,128)(2,1)S(1)}, bf16[8,1152]{1,0:T(8,128)(2,1)}, u32[]{:S(2)}) copy-start(bf16[8,1152]{1,0:T(8,128)(2,1)} %img_ref.7) | copy-start | bytes 55300
  30.1 5.6 %copy-start.1 = (bf16[8,1152]{1,0:T(8,128)(2,1)S(1)}, bf16[8,1152]{1,0:T(8,128)(2,1)}, u32[]{:S(2)}) copy-start(bf16[8,1152]{1,0:T(8,128)(2,1)} %txt_ref.7) | copy-start | bytes 55300
  30.1 21.9 %all-to-all-start = ((bf16[8,8,2304]{2,1,0:T(8,128)(2,1)}), bf16[8,8,2304]{2,1,0:T(8,128)(2,1)S(1)}, u32[]{:S(2)}, u32[]{:S(2)}) async-start(bf16[8,8,2304]{2,1,0:T(8,128)(2,1)} %bitcast.11), calls=%async_computation | async-start | bytes 589824 | tf_op jit(solution)/shard_map/all_to_all | solution.py:128
  35.7 3.2 %collective-permute-start.2 = (bf16[16,1152]{1,0:T(8,128)(2,1)S(1)}, bf16[16,1152]{1,0:T(8,128)(2,1)S(1)}, u32[]{:S(2)}, u32[]{:S(2)}) collective-permute-start(bf16[16,1152]{1,0:T(8,128)(2,1)S(1)} %mate.1), channel_id=1, source_target_pairs={{0,32},{32,0},{1,33},{33,1},{2,34},{34,2},{3,35},{35,3},{4,36},{36... | collective-permute-start | bytes 110600 | tf_op jit(solution)/shard_map/ppermute | solution.py:155
